TPU v7x, 512 devices: a whole 4x8x8 slice. The times are simulated.
512 devices in a mesh: group: 8 (over y_hi, core), shard: 64 (over x, z, y_lo).
Axes of the slice: x: 4, y: 8 (y_hi: 4, y_lo: 2; y = y_hi * 2 + y_lo), z: 8, core: 2. Of those that a mesh axis runs over, the one named last changes fastest.
Arguments:
- learner_inputs: bfloat16 [8, 8192, 8192], P('group', 'shard'), may hold values from -16 to 16
- learner_cotangent: bfloat16 [8, 8192, 4096], P('group', 'shard'), may hold values from -16 to 16
- down_factor: float32 [8192, 64], P('shard'), may hold values from -0.0625 to 0.0625
- up_factor: float32 [4096, 64], P('shard'), may hold values from -0.75 to 0.75
- weight: bfloat16 [8192, 4096], P('shard'), may hold values from -0.0625 to 0.0625
- context: bfloat16 [8, 4, 8, 8192], P('group', None, None, 'shard'), may hold values from -6 to 6
- residual: bfloat16 [8, 4, 8, 4096], P('group'), may hold values from -6 to 6
Outputs:
- new_down: bfloat16 [8192, 64], P('shard')
- new_up: bfloat16 [4096, 64], P('shard')
- decoded: bfloat16 [8, 4, 8, 4096], P('group')
All inputs are finite; a program needn't handle non-finite values.
Results may differ from a plain program's by a relative error of at most 0.008.
Values may be sent and summed in bfloat16 or wider, within the bound.
A program may use at most 64 MiB of HBM per device.

v0:
```python
import math

import jax
import jax.numpy as jnp
from jax import lax
from jax.sharding import PartitionSpec as P

MODEL_WIDTH = 8192
OUTPUT_FEATURES = 4096
ADAPTER_RANK = 64


adapter_scale = 2.0


def spread(value, axis, source):
    kept = jnp.where(lax.axis_index(axis) == source, value, 0).astype(value.dtype)
    return lax.psum(kept, axis)


def per_device(
    learner_inputs, learner_cotangent, down_factor, up_factor, weight, context, residual
):
    current_inputs = learner_inputs[0]
    output_gradient = learner_cotangent[0]
    shard_rows = down_factor.shape[0]
    up_rows = up_factor.shape[0]
    down_whole, up_whole = (
        lax.all_gather(down_factor.astype(jnp.bfloat16), "shard", axis=0, tiled=True),
        lax.all_gather(up_factor.astype(jnp.bfloat16), "shard", axis=0, tiled=True),
    )
    lowered_rows = jnp.dot(current_inputs, down_whole, preferred_element_type=jnp.float32).astype(
        jnp.bfloat16
    )
    raised_rows = jnp.dot(output_gradient, up_whole, preferred_element_type=jnp.float32).astype(
        jnp.bfloat16
    )
    down_gradient = lax.psum_scatter(
        adapter_scale
        * lax.dot_general(
            current_inputs,
            raised_rows,
            (((0,), (0,)), ((), ())),
            preferred_element_type=jnp.float32,
        ),
        "shard",
        scatter_dimension=0,
        tiled=True,
    )
    up_gradient = lax.psum_scatter(
        adapter_scale
        * lax.dot_general(
            output_gradient,
            lowered_rows,
            (((0,), (0,)), ((), ())),
            preferred_element_type=jnp.float32,
        ),
        "shard",
        scatter_dimension=0,
        tiled=True,
    )
    row_total = current_inputs.shape[0] * lax.axis_size("shard")
    down_learning_rate = (
        0.5
        * math.sqrt(ADAPTER_RANK)
        / (adapter_scale * math.sqrt(MODEL_WIDTH * OUTPUT_FEATURES) * math.sqrt(row_total))
    )
    up_learning_rate = 0.5 / (adapter_scale * math.sqrt(ADAPTER_RANK) * math.sqrt(row_total))
    down_local = (down_factor - down_learning_rate * down_gradient).astype(jnp.bfloat16)
    up_local = (up_factor - up_learning_rate * up_gradient).astype(jnp.bfloat16)
    down_all, up_all = (
        lax.all_gather(down_local, "shard", axis=0, tiled=True),
        lax.all_gather(up_local, "shard", axis=0, tiled=True),
    )
    down_all, whole_up = (spread(down_all, "group", 0), spread(up_all, "group", 0))
    position = lax.axis_index("shard")
    own_down = lax.dynamic_slice_in_dim(down_all, position * shard_rows, shard_rows, 0)
    own_up = lax.dynamic_slice_in_dim(whole_up, position * up_rows, up_rows, 0)
    weight_delta = lax.dot_general(
        own_down, whole_up, (((1,), (1,)), ((), ())), preferred_element_type=jnp.float32
    )
    combined_weight = (weight.astype(jnp.float32) + adapter_scale * weight_delta).astype(
        jnp.bfloat16
    )
    own_context = context[0]
    step_sums = []
    for decode_step in range(own_context.shape[0]):
        partial_sum = jnp.dot(
            own_context[decode_step], combined_weight, preferred_element_type=jnp.float32
        )
        step_sums.append(lax.psum(partial_sum, "shard"))
    projected = jnp.stack(step_sums)
    decoded = (residual[0].astype(jnp.float32) + projected).astype(jnp.bfloat16)
    return (own_down, own_up, decoded[None])


def solution(mesh):
    placed = (
        P("group", "shard", None),
        P("group", "shard", None),
        P("shard", None),
        P("shard", None),
        P("shard", None),
        P("group", None, None, "shard"),
        P("group", None, None, None),
    )
    return jax.shard_map(
        per_device,
        mesh=mesh,
        in_specs=placed,
        out_specs=(P("shard", None), P("shard", None), P("group", None, None, None)),
        check_vma=False,
    )
```

profile of v0, /device:TPU:56, one launch (start us, length us, event | category | flops | bytes accessed | tf_op | source)
XLA Modules:
  0.0 2149.6 jit_solution(9221157280775135550)
XLA Ops:
  7.2 0.9 convert_element_type.36
  8.1 166.1 %all_gather.12 = bf16[4096,64]{1,0:T(8,128)(2,1)S(1)} all-gather(bf16[64,64]{1,0:T(8,128)(2,1)S(1)} %convert_element_type.36), channel_id=1, replica_groups=mesh['group'=8,'shard'=64] {'shard'}, dimensions={0}, use_global_device_ids=true | all-gather | bytes 532480 | tf_op jit(solution)/shard_map/all_gather | solution.py:30
  174.2 3.5 fusion
  177.7 0.0 all-gather.5.cloned.1.call-start
  177.7 315.7 %reduce-scatter.5.cloned.1.call-done = f32[128,64]{0,1:T(8,128)} async-done(((f32[8192,64]{0,1:T(8,128)}), f32[128,64]{0,1:T(8,128)}) %reduce-scatter.5.cloned.1.call-update) | async-done | bytes 32784 | tf_op jit(solution)/shard_map/reduce_scatter | solution.py:38
  493.5 1.4 fusion.24
  494.9 0.0 all-gather.3.cloned.1.call-start
  494.9 0.7 all-gather.3.cloned.1.call-update
  495.6 0.0 reduce-scatter.7.cloned.1.call-start
  495.7 231.6 %all-gather.5.cloned.1.call-done = bf16[8192,64]{0,1:T(8,128)(2,1)} async-done(((bf16[128,64]{0,1:T(8,128)(2,1)}), bf16[8192,64]{0,1:T(8,128)(2,1)}) %all-gather.5.cloned.1.call-update) | async-done | bytes 1048592 | tf_op jit(solution)/shard_map/all_gather | solution.py:29
  727.2 2.8 fusion.3
  730.1 1.9 copy.14
  732.0 0.0 all-reduce.7.cloned.1.call-start
  732.1 0.1 copy.12
  732.2 229.1 %all-gather.3.cloned.1.call-done = bf16[8192,64]{0,1:T(8,128)(2,1)} async-done(((bf16[128,64]{0,1:T(8,128)(2,1)}), bf16[8192,64]{0,1:T(8,128)(2,1)}) %all-gather.3.cloned.1.call-update) | async-done | bytes 1048592 | tf_op jit(solution)/shard_map/all_gather | solution.py:72
  961.2 1.0 broadcast_select_fusion.1
  962.3 316.5 %reduce-scatter.7.cloned.1.call-done = f32[64,64]{1,0:T(8,128)} async-done(((f32[4096,64]{1,0:T(8,128)}), f32[64,64]{1,0:T(8,128)}) %reduce-scatter.7.cloned.1.call-update) | async-done | bytes 16400
  1278.8 0.8 copy.15
  1279.7 0.1 copy.13
  1279.7 163.5 %all_gather.15 = bf16[4096,64]{1,0:T(8,128)(2,1)S(1)} all-gather(bf16[64,64]{1,0:T(8,128)(2,1)S(1)} %copy.13), channel_id=1, replica_groups=mesh['group'=8,'shard'=64] {'shard'}, dimensions={0}, use_global_device_ids=true | all-gather | bytes 532480 | tf_op jit(solution)/shard_map/all_gather | solution.py:73
  1443.2 1.1 broadcast_select_fusion
  1444.3 0.0 all-reduce.5.cloned.1.call-start
  1444.4 80.6 %all-reduce.7.cloned.1.call-done = (bf16[8192,64]{0,1:T(8,128)(2,1)}, bf16[4096,64]{1,0:T(8,128)(2,1)}) async-done(((bf16[8192,64]{0,1:T(8,128)(2,1)}, bf16[4096,64]{1,0:T(8,128)(2,1)}), (bf16[8192,64]{0,1:T(8,128)(2,1)}, bf16[4096,64]{1,0:T(8,128)(2,1)})) %all-reduce.7.cloned.1.call-update) | async-done | bytes 1572880 | tf_op jit(solution)/shard_map/psum | solution.py:18
  1524.9 0.7 constant_dynamic-slice_fusion.1
  1525.7 1.7 fusion.2
  1527.4 0.9 convolution_bitcast_fusion
  1528.3 0.9 convolution_bitcast_fusion.1
  1529.2 0.9 convolution_bitcast_fusion.2
  1530.1 0.9 convolution_bitcast_fusion.3
  1531.0 1.3 constant_dynamic-slice_fusion
  1532.4 608.6 %all-reduce.5.cloned.1.call-done = (f32[1,1,8,4096]{3,2,1,0:T(8,128)}, f32[1,1,8,4096]{3,2,1,0:T(8,128)}, f32[1,1,8,4096]{3,2,1,0:T(8,128)}, f32[1,1,8,4096]{3,2,1,0:T(8,128)}) async-done(((f32[1,1,8,4096]{3,2,1,0:T(8,128)}, f32[1,1,8,4096]{3,2,1,0:T(8,128)}, f32[1,1,8,4096]{3,2,1,0:T(8,128)}, f32[1,1,8,4096]{3,2,1,0:T(8,128)}), (f32[1,1,8,4096]{3,2,1,0:T(8,128)}, f32[1,1,8,4096]{3,2,1,0:T(8,128)}, ...) | async-done | bytes 524304 | tf_op jit(solution)/shard_map/psum | solution.py:91
  2140.9 1.8 fusion.15
  (21 shorter events, 0.2 us)
Async XLA Ops:
  7.2 167.0 %copy-start = (bf16[1,128,8192]{2,1,0:T(8,128)(2,1)S(1)}, bf16[1,128,8192]{2,1,0:T(8,128)(2,1)}, u32[]{:S(2)}) copy-start(bf16[1,128,8192]{2,1,0:T(8,128)(2,1)} %param.7) | copy-start | bytes 6291460
  7.2 486.3 %reduce-scatter.5.cloned.1.call-start = ((), (), s32[]{:S(2)}) async-start(), calls=%async_computation.2 | async-start | bytes 2129920 | tf_op jit(solution)/shard_map/reduce_scatter | solution.py:38
  177.7 315.8 %copy-start.5 = (f32[128,64]{0,1:T(8,128)S(1)}, f32[128,64]{0,1:T(8,128)}, u32[]{:S(2)}) copy-start(f32[128,64]{0,1:T(8,128)} %param.9) | copy-start | bytes 98308
  177.7 549.6 %all-gather.5.cloned.1.call-start = ((), (), s32[]{:S(2)}) async-start(), calls=%async_computation.4 | async-start | bytes 1064960 | tf_op jit(solution)/shard_map/all_gather | solution.py:29
  494.9 466.3 %all-gather.3.cloned.1.call-start = ((), (), s32[]{:S(2)}) async-start(), calls=%async_computation.3 | async-start | bytes 1064960 | tf_op jit(solution)/shard_map/all_gather | solution.py:72
  495.6 783.2 %reduce-scatter.7.cloned.1.call-start = ((), (), s32[]{:S(2)}) async-start(), calls=%async_computation.5 | async-start | bytes 2129920
  730.1 2.0 copy-start.3
  732.0 792.9 %all-reduce.7.cloned.1.call-start = ((), (), s32[]{:S(2)}) async-start(), calls=%async_computation.7 | async-start | bytes 4194304 | tf_op jit(solution)/shard_map/psum | solution.py:18
  1443.2 82.5 %copy-start.1 = (bf16[128,4096]{1,0:T(8,128)(2,1)S(1)}, bf16[128,4096]{1,0:T(8,128)(2,1)}, u32[]{:S(2)}) copy-start(bf16[128,4096]{1,0:T(8,128)(2,1)} %param.11) | copy-start | bytes 3145732
  1444.3 83.1 %copy-start.6 = (bf16[1,4,8,128]{3,2,1,0:T(8,128)(2,1)S(1)}, bf16[1,4,8,128]{3,2,1,0:T(8,128)(2,1)}, u32[]{:S(2)}) copy-start(bf16[1,4,8,128]{3,2,1,0:T(8,128)(2,1)} %param.12) | copy-start | bytes 24580
  1444.3 696.6 %all-reduce.5.cloned.1.call-start = ((), (), s32[]{:S(2)}) async-start(), calls=%async_computation.6 | async-start | bytes 1048576 | tf_op jit(solution)/shard_map/psum | solution.py:91
  1525.7 2.6 copy-start.4
  1528.3 612.6 %copy-start.2 = (bf16[1,4,8,4096]{3,2,1,0:T(8,128)(2,1)S(1)}, bf16[1,4,8,4096]{3,2,1,0:T(8,128)(2,1)}, u32[]{:S(2)}) copy-start(bf16[1,4,8,4096]{3,2,1,0:T(8,128)(2,1)} %param.13) | copy-start | bytes 786436
Sparse Core Ops, SparseCore 0:
  177.8 315.6 reduce-scatter.4
  496.3 230.9 all-gather.4
  730.0 231.1 all-gather.2
  964.1 314.6 reduce-scatter.6
  1444.4 80.4 all-reduce.6
  1531.2 609.7 all-reduce.4
where the time goes:
time: 2150 us
  waiting for transfers between devices  1780 us (83%)
  blocking collectives  330 us (15%)
    psum x1, waiting for transfers between devices, per_device(): step_sums.append(lax.psum(partial_sum, 'shard'))  609 us
    unnamed x7, waiting for transfers between devices  317 us
    reduce_scatter x1, waiting for transfers between devices, per_device(): lax.psum_scatter(adapter_scale * lax.dot_general(current_inputs, raised_r...  316 us
    all_gather x1, waiting for transfers between devices, per_device(): lax.all_gather(down_factor.astype(jnp.bfloat16), 'shard', axis=0, tiled=T...  232 us
    all_gather x1, waiting for transfers between devices, per_device(): lax.all_gather(down_local, 'shard', axis=0, tiled=True)  229 us
    all_gather x1, blocking collectives, per_device(): lax.all_gather(up_factor.astype(jnp.bfloat16), 'shard', axis=0, tiled=True)  166 us
    all_gather x1, blocking collectives, per_device(): lax.all_gather(up_local, 'shard', axis=0, tiled=True)  163 us
    psum x1, waiting for transfers between devices, spread(): return lax.psum(kept, axis)  80.6 us
  transfers between devices with their start and end apart: 6, of which 6 were waited for; matrix products, arithmetic and copies ran while one was open for 0% of the time, Pallas kernels for 0%

commit v1 on v0

v1 whole, which is shorter than its diff:
```python
import functools
import math

import jax
import jax.numpy as jnp
from jax import lax
from jax.experimental import pallas as pl
from jax.experimental.pallas import tpu as pltpu
from jax.sharding import PartitionSpec as P

RANK = 64
SCALE = 2.0
F32 = jnp.float32
BF16 = jnp.bfloat16
NT = (((1,), (1,)), ((), ()))


def torus(shards):
    return {64: (4, 8, 2), 8: (2, 2, 2)}[shards]


def left_half(shape):
    return lax.broadcasted_iota(jnp.int32, shape, 1) < 64


def halves(even, odd):
    keep = left_half(even.shape)
    first = jnp.where(keep, even, pltpu.roll(odd, 64, 1))
    second = jnp.where(keep, pltpu.roll(even, 64, 1), odd)
    return first, second


def kernel(
    sizes, rates,
    x_hbm, c_hbm, down_hbm, up_hbm, w_hbm, ctx_hbm, res_hbm,
    new_ref, dec_ref,
    x_v, c_v, down_v, up_v, w_v, ctx_v, res_v,
    ag, grads, a1, a1s, a2, a2s, a3, b1, b1s, b2, b2s, b3,
    base, p1, p1s, p2, p2s, p3, fresh, tz, tx, ty, txs, tys, outs,
    local_sem, send_sem, recv_sem,
):
    nx, nz, ny, groups = sizes
    group = lax.axis_index("group")
    shard = lax.axis_index("shard")
    y = lax.rem(shard, ny)
    z = lax.rem(shard // ny, nz)
    x = shard // (ny * nz)
    learner = group == 0
    tokens = x_v.shape[0]

    def at(xx, zz, yy):
        return (xx * nz + zz) * ny + yy

    def x_peer(d):
        return lax.rem(x + d, nx)

    def z_peer(d):
        return lax.rem(z + d, nz)

    other = 1 - y

    local = [
        pltpu.make_async_copy(src, dst, local_sem.at[i])
        for i, (src, dst) in enumerate(
            [
                (down_hbm, down_v),
                (up_hbm, up_v),
                (ctx_hbm, ctx_v),
                (w_hbm, w_v),
                (res_hbm.at[:, pl.ds(pl.multiple_of((shard // ny) * 128, 128), 128)], res_v),
                (c_hbm, c_v),
                (x_hbm, x_v),
            ]
        )
    ]
    for copy in local[:5]:
        copy.start()

    @pl.when(learner)
    def _():
        local[5].start()
        local[6].start()

    barrier = pltpu.get_barrier_semaphore()
    peers = (
        [at(x, z_peer(d), y) for d in range(1, nz)]
        + [at(x_peer(d), z, y) for d in range(1, nx)]
        + [at(x, z, other)]
    )
    for peer in peers:
        pl.semaphore_signal(
            barrier, inc=1, device_id={"shard": peer}, device_id_type=pl.DeviceIdType.MESH
        )

    @pl.when(jnp.logical_not(learner))
    def _():
        pl.semaphore_signal(
            barrier, inc=1, device_id={"group": 0}, device_id_type=pl.DeviceIdType.MESH
        )

    pl.semaphore_wait(barrier, len(peers) + jnp.where(learner, groups - 1, 0))

    used = [0]

    def remote(src, dst, peer):
        k = used[0]
        used[0] += 1
        return pltpu.make_async_remote_copy(
            src_ref=src, dst_ref=dst, send_sem=send_sem.at[k], recv_sem=recv_sem.at[k],
            device_id={"shard": peer}, device_id_type=pl.DeviceIdType.MESH,
        )

    def start(copies):
        for copy in copies:
            copy.start()

    def arrive(copies):
        for copy in copies:
            copy.wait_recv()

    gz = [remote(ag.at[y, x, z], ag.at[y, x, z], at(x, z_peer(d), y)) for d in range(1, nz)]
    gax = [
        remote(ag.at[y, x, :, 0:48], ag.at[y, x, :, 0:48], at(x_peer(d), z, y))
        for d in range(1, nx)
    ]
    gay = [remote(ag.at[y, :, :, 0:48], ag.at[y, :, :, 0:48], at(x, z, other))]
    gby = [remote(ag.at[y, x, :, 48:96], ag.at[y, x, :, 48:96], at(x, z, other))]
    gbx = [
        remote(ag.at[:, x, :, 48:96], ag.at[:, x, :, 48:96], at(x_peer(d), z, y))
        for d in range(1, nx)
    ]
    ray = [remote(grads.at[other, :, :, 0:48], a1, at(x, z, other))]
    rax = [remote(a1s.at[x_peer(d)], a2.at[d - 1], at(x_peer(d), z, y)) for d in range(1, nx)]
    raz = [remote(a2s.at[z_peer(d)], a3.at[d - 1], at(x, z_peer(d), y)) for d in range(1, nz)]
    rbx = [
        remote(grads.at[:, x_peer(d), :, 48:96], b1.at[d - 1], at(x_peer(d), z, y))
        for d in range(1, nx)
    ]
    rby = [remote(b1s.at[other], b2, at(x, z, other))]
    rbz = [remote(b2s.at[z_peer(d)], b3.at[d - 1], at(x, z_peer(d), y)) for d in range(1, nz)]
    py = [remote(base.at[other], p1, at(x, z, other))]
    px = [remote(p1s.at[x_peer(d)], p2.at[d - 1], at(x_peer(d), z, y)) for d in range(1, nx)]
    pz = [remote(p2s.at[z_peer(d)], p3.at[d - 1], at(x, z_peer(d), y)) for d in range(1, nz)]
    sz = [remote(tz.at[0], tz.at[d], at(x, z_peer(d), y)) for d in range(1, nz)]
    sx = [remote(tx.at[0], tx.at[d], at(x_peer(d), z, y)) for d in range(1, nx)]
    sy = [remote(ty.at[0], ty.at[1], at(x, z, other))]
    oz = [remote(outs.at[y, x, z], outs.at[y, x, z], at(x, z_peer(d), y)) for d in range(1, nz)]
    ox = [remote(outs.at[y, x], outs.at[y, x], at(x_peer(d), z, y)) for d in range(1, nx)]
    oy = [remote(outs.at[y], outs.at[y], at(x, z, other))]
    k_group = used[0]
    spread = [
        pltpu.make_async_remote_copy(
            src_ref=fresh, dst_ref=fresh, send_sem=send_sem.at[k_group + g - 1],
            recv_sem=recv_sem.at[k_group],
            device_id={"group": g}, device_id_type=pl.DeviceIdType.MESH,
        )
        for g in range(1, groups)
    ]

    def factors():
        down_t = down_v[...].T
        up_t = up_v[...].T
        up_t = jnp.concatenate([up_t, jnp.zeros_like(up_t)], axis=1)
        packed, _ = halves(up_t[0:32], up_t[32:64])
        return down_t, packed

    local[0].wait()
    local[1].wait()

    @pl.when(learner)
    def _():
        down_t, packed = factors()
        ag[y, x, z, 0:64] = down_t.astype(BF16)
        ag[y, x, z, 64:96] = packed.astype(BF16)
        start(gz)

    local[2].wait()
    local[3].wait()

    def project(xx, _):
        for zz in range(nz):
            column = pl.multiple_of((xx * nz + zz) * 128, 128)
            block = jnp.dot(ctx_v[...], w_v[:, pl.ds(column, 128)], preferred_element_type=F32)
            even, odd = halves(block[0:16], block[16:32])
            base[0, xx, zz] = even.astype(BF16)
            base[1, xx, zz] = odd.astype(BF16)
        return 0

    lax.fori_loop(0, nx, project, 0)

    @pl.when(jnp.logical_not(learner))
    def _():
        start(py)

    @pl.when(learner)
    def _():
        arrive(gz)
        start(gax)
        start(gby)
        start(py)
        arrive(gax)
        start(gay)
        arrive(gby)
        start(gbx)

    arrive(py)
    p1s[...] = (base[y].astype(F32) + p1[...].astype(F32)).astype(BF16)
    start(px)
    arrive(px)
    total = p1s[x].astype(F32)
    for d in range(1, nx):
        total = total + p2[d - 1].astype(F32)
    p2s[...] = total.astype(BF16)
    start(pz)

    @pl.when(learner)
    def _():
        local[5].wait()
        arrive(gbx)

        def lift(xx, total):
            for zz in range(nz):
                column = pl.multiple_of((xx * nz + zz) * 128, 128)
                even = ag[0, xx, zz, 64:96].astype(F32)
                odd = ag[1, xx, zz, 64:96].astype(F32)
                top, low = halves(even, odd)
                up_t = jnp.concatenate([top, low], axis=0).astype(BF16)
                total = total + lax.dot_general(
                    up_t, c_v[:, pl.ds(column, 128)], NT, preferred_element_type=F32
                )
            return total

        lifted = lax.fori_loop(0, nx, lift, jnp.zeros((RANK, tokens), F32)).astype(BF16)
        local[6].wait()

        def down_grads(xx, _):
            for zz in range(nz):
                column = pl.multiple_of((xx * nz + zz) * 256, 256)
                block = jnp.dot(lifted, x_v[:, pl.ds(column, 256)], preferred_element_type=F32)
                block = block.astype(BF16)
                grads[0, xx, zz, 0:64] = block[:, 0:128]
                grads[1, xx, zz, 0:64] = block[:, 128:256]
            return 0

        lax.fori_loop(0, nx, down_grads, 0)
        start(ray)
        arrive(gay)

        def lower(xx, total):
            for zz in range(nz):
                column = pl.multiple_of((xx * nz + zz) * 256, 256)
                down_t = jnp.concatenate([ag[0, xx, zz, 0:64], ag[1, xx, zz, 0:64]], axis=1)
                total = total + lax.dot_general(
                    down_t, x_v[:, pl.ds(column, 256)], NT, preferred_element_type=F32
                )
            return total

        lowered = lax.fori_loop(0, nx, lower, jnp.zeros((RANK, tokens), F32)).astype(BF16)

        def up_grads(xx, _):
            for zz in range(nz):
                column = pl.multiple_of((xx * nz + zz) * 128, 128)
                block = jnp.dot(lowered, c_v[:, pl.ds(column, 128)], preferred_element_type=F32)
                even, odd = halves(block[0:32], block[32:64])
                grads[0, xx, zz, 64:96] = even.astype(BF16)
                grads[1, xx, zz, 64:96] = odd.astype(BF16)
            return 0

        lax.fori_loop(0, nx, up_grads, 0)
        start(rbx)
        arrive(ray)
        a1s[...] = (grads[y, :, :, 0:48].astype(F32) + a1[...].astype(F32)).astype(BF16)
        start(rax)
        arrive(rbx)
        total = grads[:, x, :, 48:96].astype(F32)
        for d in range(1, nx):
            total = total + b1[d - 1].astype(F32)
        b1s[...] = total.astype(BF16)
        start(rby)
        arrive(rax)
        total = a1s[x].astype(F32)
        for d in range(1, nx):
            total = total + a2[d - 1].astype(F32)
        a2s[...] = total.astype(BF16)
        start(raz)
        arrive(rby)
        b2s[...] = (b1s[y].astype(F32) + b2[...].astype(F32)).astype(BF16)
        start(rbz)
        arrive(raz)
        down_t, packed = factors()
        total = a2s[z].astype(F32)
        for d in range(1, nz):
            total = total + a3[d - 1].astype(F32)
        fresh[0:48] = (down_t[0:48] - rates[0] * (SCALE * total)).astype(BF16)
        arrive(rbz)
        total = b2s[z].astype(F32)
        for d in range(1, nz):
            total = total + b3[d - 1].astype(F32)
        fresh[48:64] = (down_t[48:64] - rates[0] * (SCALE * total[0:16])).astype(BF16)
        fresh[64:96] = (packed - rates[1] * (SCALE * total[16:48])).astype(BF16)
        start(spread)

    arrive(pz)
    frozen = p2s[z].astype(F32)
    for d in range(1, nz):
        frozen = frozen + p3[d - 1].astype(F32)
    local[4].wait()
    even, odd = halves(res_v[0:16].astype(F32), res_v[16:32].astype(F32))
    frozen = frozen + jnp.where(y == 0, even, odd)

    @pl.when(jnp.logical_not(learner))
    def _():
        spread[0].wait_recv()

    new_down = fresh[0:64]
    nothing = jnp.zeros_like(new_down)
    first = jnp.concatenate([new_down, nothing], axis=0)
    second = jnp.concatenate([nothing, new_down], axis=0)
    tz[0] = lax.dot_general(
        ctx_v[0:16], first, NT, preferred_element_type=F32
    ) + lax.dot_general(ctx_v[16:32], second, NT, preferred_element_type=F32)
    start(sz)
    arrive(sz)
    tx[0] = jnp.sum(tz[...], axis=0)
    start(sx)
    arrive(sx)
    ty[0] = jnp.sum(tx[...], axis=0)
    start(sy)
    arrive(sy)
    lowered_rows = (ty[0] + ty[1]).astype(BF16)
    packed = fresh[64:96].astype(F32)
    turned = pltpu.roll(packed, 64, 1)
    keep = left_half(packed.shape)
    square = jnp.concatenate(
        [
            jnp.where(keep, packed, 0.0),
            jnp.where(keep, turned, 0.0),
            jnp.where(keep, 0.0, turned),
            jnp.where(keep, 0.0, packed),
        ],
        axis=0,
    ).astype(BF16)
    delta = jnp.dot(lowered_rows, square, preferred_element_type=F32)
    outs[y, x, z] = (frozen + SCALE * delta).astype(BF16)
    start(oz)
    new_ref[...] = fresh[...]
    arrive(oz)
    start(ox)
    arrive(ox)
    start(oy)
    arrive(oy)

    def unpack(xx, _):
        for zz in range(nz):
            column = pl.multiple_of((xx * nz + zz) * 128, 128)
            top, low = halves(outs[0, xx, zz].astype(F32), outs[1, xx, zz].astype(F32))
            dec_ref[0:16, pl.ds(column, 128)] = top.astype(BF16)
            dec_ref[16:32, pl.ds(column, 128)] = low.astype(BF16)
        return 0

    lax.fori_loop(0, nx, unpack, 0)

    for copy in py + px + pz + sz + sx + sy + oz + ox + oy:
        copy.wait_send()

    @pl.when(learner)
    def _():
        for copy in gz + gax + gay + gby + gbx + ray + rax + raz + rbx + rby + rbz + spread:
            copy.wait_send()


def per_device(
    sizes, rates,
    learner_inputs, learner_cotangent, down_factor, up_factor, weight, context, residual
):
    nx, nz, ny, groups = sizes
    tokens, width = learner_inputs.shape[1:]
    features = learner_cotangent.shape[2]
    rows = context.shape[1] * context.shape[2]
    copies = 7 * (nz - 1) + 7 * (nx - 1) + 7 + (groups - 1)
    scratch = [
        pltpu.VMEM((tokens, width), BF16),
        pltpu.VMEM((tokens, features), BF16),
        pltpu.VMEM(down_factor.shape, F32),
        pltpu.VMEM(up_factor.shape, F32),
        pltpu.VMEM(weight.shape, BF16),
        pltpu.VMEM((rows, 128), BF16),
        pltpu.VMEM((rows, 128), BF16),
        pltpu.VMEM((ny, nx, nz, 96, 128), BF16),
        pltpu.VMEM((ny, nx, nz, 96, 128), BF16),
        pltpu.VMEM((nx, nz, 48, 128), BF16),
        pltpu.VMEM((nx, nz, 48, 128), BF16),
        pltpu.VMEM((nx - 1, nz, 48, 128), BF16),
        pltpu.VMEM((nz, 48, 128), BF16),
        pltpu.VMEM((nz - 1, 48, 128), BF16),
        pltpu.VMEM((nx - 1, ny, nz, 48, 128), BF16),
        pltpu.VMEM((ny, nz, 48, 128), BF16),
        pltpu.VMEM((nz, 48, 128), BF16),
        pltpu.VMEM((nz, 48, 128), BF16),
        pltpu.VMEM((nz - 1, 48, 128), BF16),
        pltpu.VMEM((ny, nx, nz, 16, 128), BF16),
        pltpu.VMEM((nx, nz, 16, 128), BF16),
        pltpu.VMEM((nx, nz, 16, 128), BF16),
        pltpu.VMEM((nx - 1, nz, 16, 128), BF16),
        pltpu.VMEM((nz, 16, 128), BF16),
        pltpu.VMEM((nz - 1, 16, 128), BF16),
        pltpu.VMEM((96, 128), BF16),
        pltpu.VMEM((nz, 16, 128), F32),
        pltpu.VMEM((nx, 16, 128), F32),
        pltpu.VMEM((ny, 16, 128), F32),
        pltpu.VMEM((16, 128), F32),
        pltpu.VMEM((16, 128), F32),
        pltpu.VMEM((ny, nx, nz, 16, 128), BF16),
        pltpu.SemaphoreType.DMA((7,)),
        pltpu.SemaphoreType.DMA((copies,)),
        pltpu.SemaphoreType.DMA((copies,)),
    ]
    fresh, decoded = pl.pallas_call(
        functools.partial(kernel, sizes, rates),
        out_shape=(
            jax.ShapeDtypeStruct((96, 128), BF16),
            jax.ShapeDtypeStruct((rows, features), BF16),
        ),
        in_specs=[pl.BlockSpec(memory_space=pl.ANY)] * 7,
        out_specs=(pl.BlockSpec(memory_space=pltpu.VMEM),) * 2,
        scratch_shapes=scratch,
        compiler_params=pltpu.CompilerParams(
            collective_id=0, has_side_effects=True, vmem_limit_bytes=40 * 1024 * 1024
        ),
        name="lora_step",
    )(
        learner_inputs[0], learner_cotangent[0], down_factor, up_factor, weight,
        context[0].reshape(rows, -1), residual[0].reshape(rows, features),
    )
    new_down = fresh[0:64].T
    new_up = jnp.concatenate([fresh[64:96, 0:64], fresh[64:96, 64:128]], axis=0).T
    return new_down, new_up, decoded.reshape(residual.shape)


def solution(mesh):
    groups, shards = mesh.shape["group"], mesh.shape["shard"]
    nx, nz, ny = torus(shards)
    placed = (
        P("group", "shard", None),
        P("group", "shard", None),
        P("shard", None),
        P("shard", None),
        P("shard", None),
        P("group", None, None, "shard"),
        P("group", None, None, None),
    )

    def whole(learner_inputs, learner_cotangent, *others):
        tokens, width = learner_inputs.shape[1:]
        features = learner_cotangent.shape[2]
        rates = (
            0.5 * math.sqrt(RANK) / (SCALE * math.sqrt(width * features) * math.sqrt(tokens)),
            0.5 / (SCALE * math.sqrt(RANK) * math.sqrt(tokens)),
        )
        return jax.shard_map(
            functools.partial(per_device, (nx, nz, ny, groups), rates),
            mesh=mesh,
            in_specs=placed,
            out_specs=(P("shard", None), P("shard", None), P("group", None, None, None)),
            check_vma=False,
        )(learner_inputs, learner_cotangent, *others)

    return whole
```

time: 2150 us -> 94.5 us (0.04)
  waiting for transfers between devices: 1780 us -> 0 us
  blocking collectives: 330 us -> 0 us
  Pallas kernels: 0 us -> 83.9 us
    psum x2 -> x0, waiting for transfers between devices: 689 us -> none  [the longest x1 609 us: per_device(): step_sums.append(lax.psum(partial_sum, 'shard'))]
    all_gather x2 -> x0, waiting for transfers between devices: 461 us -> none  [the longest x1 232 us: per_device(): lax.all_gather(down_factor.astype(jnp.bfloat16), 'shard', axis=0, tiled=T...]
    all_gather x2 -> x0, blocking collectives: 330 us -> none  [the longest x1 166 us: per_device(): lax.all_gather(up_factor.astype(jnp.bfloat16), 'shard', axis=0, tiled=True)]
    unnamed x7 -> x0, waiting for transfers between devices: 317 us -> none
    reduce_scatter x1 -> x0, waiting for transfers between devices: 316 us -> none  [per_device(): lax.psum_scatter(adapter_scale * lax.dot_general(current_inputs, raised_r...]
    pallas_call x0 -> x1, Pallas kernels: none -> 83.9 us  [per_device(): pl.pallas_call(functools.partial(kernel, sizes, rates), out_shape=(jax.Sh...]
  transfers between devices with their start and end apart: 6 -> 0, of which waited for: 6 -> 0; matrix products, arithmetic and copies ran while one was open for 0% -> 0% of each run, Pallas kernels for 0% -> 0%
where the time goes in v1:
time: 94.5 us; the launch traced here: 94 us
  Pallas kernels  83.9 us (89%)
  local copies, waits for them, and re-layouts  9.37 us (10%)
    pallas_call x1, Pallas kernels, per_device(): pl.pallas_call(functools.partial(kernel, sizes, rates), out_shape=(jax.Sh...  83.9 us
    unnamed x15, local copies, waits for them, and re-layouts  8.69 us

profile of v1, /device:TPU:56, one launch (start us, length us, event | category | flops | bytes accessed | tf_op | source)
XLA Modules:
  0.0 94.0 jit_solution(13027314570080828755)
XLA Ops:
  0.6 0.8 copy.10.down_hbm
  1.5 0.0 copy-start
  1.5 1.6 %copy-done = bf16[1,128,8192]{2,1,0:T(8,128)(2,1)S(1)} copy-done((bf16[1,128,8192]{2,1,0:T(8,128)(2,1)S(1)}, bf16[1,128,8192]{2,1,0:T(8,128)(2,1)}, u32[]{:S(2)}) %copy-start) | copy-done | bytes 2097176
  3.1 0.0 copy-start.1
  3.1 1.2 %copy-done.1 = bf16[1,128,4096]{2,1,0:T(8,128)(2,1)S(1)} copy-done((bf16[1,128,4096]{2,1,0:T(8,128)(2,1)S(1)}, bf16[1,128,4096]{2,1,0:T(8,128)(2,1)}, u32[]{:S(2)}) %copy-start.1) | copy-done | bytes 1048600
  4.3 0.0 copy-start.2
  4.3 1.2 %copy-done.2 = bf16[128,4096]{1,0:T(8,128)(2,1)S(1)} copy-done((bf16[128,4096]{1,0:T(8,128)(2,1)S(1)}, bf16[128,4096]{1,0:T(8,128)(2,1)}, u32[]{:S(2)}) %copy-start.2) | copy-done | bytes 1048600
  5.5 0.0 copy-start.3
  5.5 0.9 %copy-done.3 = bf16[1,4,8,4096]{3,2,1,0:T(8,128)(2,1)S(1)} copy-done((bf16[1,4,8,4096]{3,2,1,0:T(8,128)(2,1)S(1)}, bf16[1,4,8,4096]{3,2,1,0:T(8,128)(2,1)}, u32[]{:S(2)}) %copy-start.3) | copy-done | bytes 262168
  6.5 0.0 copy-start.4
  6.5 0.8 copy-done.4
  7.2 0.0 copy-start.5
  7.2 0.7 copy-done.5
  7.9 83.9 %lora_step.1 = (bf16[96,128]{1,0:T(8,128)(2,1)S(1)}, bf16[32,4096]{1,0:T(8,128)(2,1)S(1)}) custom-call(bf16[128,8192]{1,0:T(8,128)(2,1)S(1)} %bitcast.9, bf16[128,4096]{1,0:T(8,128)(2,1)S(1)} %bitcast.10, f32[128,64]{1,0:T(8,128)S(1)} %copy.10.down_hbm, f32[64,64]{1,0:T(8,128)S(1)} %copy-done.4, bf16[128,4096]{1,0:T(8,128)(2,1)S(1)} %copy-done.2, ...), custom_call_target="tpu_custom_call" | custom-call | tf_op jit(solution)/shard_map/lora_step/pallas_call | solution.py:418
  91.9 0.6 slice_bitcast_fusion
  92.5 0.1 fusion
  92.6 0.7 copy.11
  93.3 0.7 copy.13
  (1 shorter events, 0.0 us)
Async XLA Ops:
  1.5 1.6 %copy-start = (bf16[1,128,8192]{2,1,0:T(8,128)(2,1)S(1)}, bf16[1,128,8192]{2,1,0:T(8,128)(2,1)}, u32[]{:S(2)}) copy-start(bf16[1,128,8192]{2,1,0:T(8,128)(2,1)} %param.7) | copy-start | bytes 6291460
  3.1 1.2 %copy-start.1 = (bf16[1,128,4096]{2,1,0:T(8,128)(2,1)S(1)}, bf16[1,128,4096]{2,1,0:T(8,128)(2,1)}, u32[]{:S(2)}) copy-start(bf16[1,128,4096]{2,1,0:T(8,128)(2,1)} %param.8) | copy-start | bytes 3145732
  4.3 1.2 %copy-start.2 = (bf16[128,4096]{1,0:T(8,128)(2,1)S(1)}, bf16[128,4096]{1,0:T(8,128)(2,1)}, u32[]{:S(2)}) copy-start(bf16[128,4096]{1,0:T(8,128)(2,1)} %w_hbm.1) | copy-start | bytes 3145732
  5.5 0.9 %copy-start.3 = (bf16[1,4,8,4096]{3,2,1,0:T(8,128)(2,1)S(1)}, bf16[1,4,8,4096]{3,2,1,0:T(8,128)(2,1)}, u32[]{:S(2)}) copy-start(bf16[1,4,8,4096]{3,2,1,0:T(8,128)(2,1)} %param.13) | copy-start | bytes 786436
  6.5 0.8 copy-start.4
  7.2 0.7 copy-start.5

commit v2 on v1

v2 whole, which is shorter than its diff:
```python
import functools
import math

import jax
import jax.numpy as jnp
from jax import lax
from jax.experimental import pallas as pl
from jax.experimental.pallas import tpu as pltpu
from jax.sharding import PartitionSpec as P

RANK = 64
SCALE = 2.0
F32 = jnp.float32
BF16 = jnp.bfloat16
NT = (((1,), (1,)), ((), ()))


def torus(shards):
    return {64: (4, 8, 2), 8: (2, 2, 2)}[shards]


def left_half(shape):
    return lax.broadcasted_iota(jnp.int32, shape, 1) < 64


def halves(even, odd):
    keep = left_half(even.shape)
    first = jnp.where(keep, even, pltpu.roll(odd, 64, 1))
    second = jnp.where(keep, pltpu.roll(even, 64, 1), odd)
    return first, second


def kernel(
    sizes, rates,
    x_hbm, c_hbm, down_hbm, up_hbm, w_hbm, ctx_hbm, res_hbm,
    new_ref, dec_ref,
    x_v, c_v, down_v, up_v, w_v, ctx_v, res_v,
    up_all, down_all, up_flat, down_flat,
    gd, rd, sd, qd, gu, ru, su, qu,
    base, rb, sb, qb, fresh, tz, txy, outs,
    local_sem, send_sem, recv_sem,
):
    nx, nz, ny, groups = sizes
    group = lax.axis_index("group")
    shard = lax.axis_index("shard")
    y = lax.rem(shard, ny)
    z = lax.rem(shard // ny, nz)
    x = shard // (ny * nz)
    other = 1 - y
    learner = group == 0

    def at(xx, zz, yy):
        return (xx * nz + zz) * ny + yy

    def x_to(d):
        return lax.rem(x + d, nx)

    def z_to(d):
        return lax.rem(z + d, nz)

    def y_to(d):
        return lax.rem(y + d, ny)

    def hops(d, n):
        return min(d, n - d)

    line = sorted(range(1, nz), key=lambda d: -hops(d, nz))
    rows = sorted(range(nx), key=lambda d: -hops(d, nx))
    plane = [(dx, dy) for dx in rows for dy in (1, 0) if (dx, dy) != (0, 0)]

    local = [
        pltpu.make_async_copy(src, dst, local_sem.at[i])
        for i, (src, dst) in enumerate(
            [
                (up_hbm, up_v),
                (down_hbm, down_v),
                (ctx_hbm, ctx_v),
                (w_hbm, w_v),
                (res_hbm.at[:, pl.ds(pl.multiple_of((shard // ny) * 128, 128), 128)], res_v),
                (c_hbm, c_v),
                (x_hbm, x_v),
            ]
        )
    ]
    for copy in local[:5]:
        copy.start()

    @pl.when(learner)
    def _():
        local[5].start()
        local[6].start()

    barrier = pltpu.get_barrier_semaphore()
    peers = [at(x, z_to(d), y) for d in line] + [at(x_to(dx), z, y_to(dy)) for dx, dy in plane]
    for peer in peers:
        pl.semaphore_signal(
            barrier, inc=1, device_id={"shard": peer}, device_id_type=pl.DeviceIdType.MESH
        )

    @pl.when(jnp.logical_not(learner))
    def _():
        pl.semaphore_signal(
            barrier, inc=1, device_id={"group": 0}, device_id_type=pl.DeviceIdType.MESH
        )

    used = [0]

    def remote(src, dst, peer):
        k = used[0]
        used[0] += 1
        return pltpu.make_async_remote_copy(
            src_ref=src, dst_ref=dst, send_sem=send_sem.at[k], recv_sem=recv_sem.at[k],
            device_id={"shard": peer}, device_id_type=pl.DeviceIdType.MESH,
        )

    def along(ref_of, dst_of):
        return [remote(ref_of(z_to(d)), dst_of(i, d), at(x, z_to(d), y)) for i, d in enumerate(line)]

    def across(ref_of, dst_of):
        return [
            remote(ref_of(x_to(dx), y_to(dy)), dst_of(i), at(x_to(dx), z, y_to(dy)))
            for i, (dx, dy) in enumerate(plane)
        ]

    def start(copies, started):
        for copy in copies:
            copy.start()
        started.extend(copies)

    def arrive(copies):
        for copy in copies:
            copy.wait_recv()

    def sent(started):
        for copy in started:
            copy.wait_send()

    learnt, decoded = [], []

    up_z = along(lambda zz: up_all.at[y, x, z], lambda i, d: up_all.at[y, x, z])
    up_xy = [
        across(lambda xx, yy: up_all.at[y, x, zz], lambda i: up_all.at[y, x, zz])
        for zz in [z] + [lax.rem(z + nz - d, nz) for d in line[::-1]]
    ]
    down_z = along(lambda zz: down_all.at[y, x, z], lambda i, d: down_all.at[y, x, z])
    down_xy = across(lambda xx, yy: down_all.at[y, x], lambda i: down_all.at[y, x])
    gd_xy = across(lambda xx, yy: gd.at[yy, xx], lambda i: rd.at[i])
    gd_z = along(lambda zz: sd.at[zz], lambda i, d: qd.at[i])
    gu_xy = across(lambda xx, yy: gu.at[yy, xx], lambda i: ru.at[i])
    gu_z = along(lambda zz: su.at[zz], lambda i, d: qu.at[i])
    base_xy = across(lambda xx, yy: base.at[yy, xx], lambda i: rb.at[i])
    base_z = along(lambda zz: sb.at[zz], lambda i, d: qb.at[i])
    low_z = along(lambda zz: tz.at[0], lambda i, d: tz.at[i + 1])
    low_xy = across(lambda xx, yy: txy.at[0], lambda i: txy.at[i + 1])
    out_z = along(lambda zz: outs.at[y, x, z], lambda i, d: outs.at[y, x, z])
    out_xy = across(lambda xx, yy: outs.at[y, x], lambda i: outs.at[y, x])

    def spread(part, k):
        order = [g for hi in (2, 1, 3, 0) for g in (2 * hi, 2 * hi + 1) if 0 < g < groups]
        return [
            pltpu.make_async_remote_copy(
                src_ref=part, dst_ref=part, send_sem=send_sem.at[k + i], recv_sem=recv_sem.at[k],
                device_id={"group": g}, device_id_type=pl.DeviceIdType.MESH,
            )
            for i, g in enumerate(order)
        ]

    down_spread = spread(fresh.at[0:64], used[0])
    up_spread = spread(fresh.at[64:96], used[0] + groups - 1)

    def summed(own, others, index=()):
        total = own.astype(F32)
        for i in range(others.shape[0]):
            total = total + others[(i, *index)].astype(F32)
        return total

    def packed_up():
        up_t = up_v[...].T
        up_t = jnp.concatenate([up_t, jnp.zeros_like(up_t)], axis=1)
        return halves(up_t[0:32], up_t[32:64])[0]

    def project(xx, _):
        for zz in range(nz):
            column = pl.multiple_of((xx * nz + zz) * 128, 128)
            block = jnp.dot(ctx_v[...], w_v[:, pl.ds(column, 128)], preferred_element_type=F32)
            even, odd = halves(block[0:16], block[16:32])
            base[0, xx, zz] = even.astype(BF16)
            base[1, xx, zz] = odd.astype(BF16)
        return 0

    def base_lines():
        arrive(base_xy)
        for d, copy in zip(line, base_z):
            zz = z_to(d)
            sb[zz] = summed(base[y, x, zz], rb, (zz,)).astype(BF16)
            copy.start()
        sb[z] = summed(base[y, x, z], rb, (z,)).astype(BF16)

    local[0].wait()
    packed = packed_up()
    pl.semaphore_wait(barrier, len(peers) + jnp.where(learner, groups - 1, 0))

    @pl.when(learner)
    def _():
        up_all[y, x, z] = packed.astype(BF16)
        start(up_z, learnt)
        start(up_xy[0], learnt)
        local[1].wait()
        down_all[y, x, z] = down_v[...].astype(BF16)
        for copy, onward in zip(up_z[::-1], up_xy[1:]):
            arrive([copy])
            start(onward, learnt)
        start(down_z, learnt)

    @pl.when(jnp.logical_not(learner))
    def _():
        local[1].wait()

    local[2].wait()
    local[3].wait()
    lax.fori_loop(0, nx, project, 0)

    @pl.when(jnp.logical_not(learner))
    def _():
        start(base_xy, [])
        base_lines()

    @pl.when(learner)
    def _():
        arrive(down_z)
        start(down_xy, learnt)
        local[5].wait()
        for copies in up_xy:
            arrive(copies)

        def unpack_up(xx, _):
            for zz in range(nz):
                column = pl.multiple_of((xx * nz + zz) * 128, 128)
                top, low = halves(
                    up_all[0, xx, zz].astype(F32), up_all[1, xx, zz].astype(F32)
                )
                up_flat[:, pl.ds(column, 128)] = jnp.concatenate([top, low], axis=0).astype(BF16)
            return 0

        lax.fori_loop(0, nx, unpack_up, 0)
        lifted = lax.dot_general(
            up_flat[...], c_v[...], NT, preferred_element_type=F32
        ).astype(BF16)
        local[6].wait()
        for dx in rows:
            xx = x_to(dx)
            for zz in range(nz):
                column = pl.multiple_of((xx * nz + zz) * 256, 256)
                block = jnp.dot(lifted, x_v[:, pl.ds(column, 256)], preferred_element_type=F32)
                block = block.astype(BF16)
                gd[0, xx, zz] = block[:, 0:128]
                gd[1, xx, zz] = block[:, 128:256]
            start([c for c, p in zip(gd_xy, plane) if p[0] == dx], learnt)
        start(base_xy, [])
        arrive(down_xy)

        def flatten(xx, _):
            for zz in range(nz):
                column = pl.multiple_of((xx * nz + zz) * 256, 256)
                down_flat[:, pl.ds(column, 256)] = jnp.concatenate(
                    [down_all[0, xx, zz], down_all[1, xx, zz]], axis=1
                )
            return 0

        lax.fori_loop(0, nx, flatten, 0)
        lowered = lax.dot_general(
            down_flat[...], x_v[...], NT, preferred_element_type=F32
        ).astype(BF16)
        for dx in rows:
            xx = x_to(dx)
            for zz in range(nz):
                column = pl.multiple_of((xx * nz + zz) * 128, 128)
                block = jnp.dot(lowered, c_v[:, pl.ds(column, 128)], preferred_element_type=F32)
                even, odd = halves(block[0:32], block[32:64])
                gu[0, xx, zz] = even.astype(BF16)
                gu[1, xx, zz] = odd.astype(BF16)
            start([c for c, p in zip(gu_xy, plane) if p[0] == dx], learnt)
        arrive(gd_xy)
        for d, copy in zip(line, gd_z):
            zz = z_to(d)
            sd[zz] = summed(gd[y, x, zz], rd, (zz,)).astype(BF16)
            start([copy], learnt)
        sd[z] = summed(gd[y, x, z], rd, (z,)).astype(BF16)
        base_lines()
        arrive(gd_z)
        total = summed(sd[z], qd)
        fresh[0:64] = (down_v[...] - rates[0] * (SCALE * total)).astype(BF16)
        start(down_spread, learnt)

    decoded.extend(base_xy + base_z)

    @pl.when(jnp.logical_not(learner))
    def _():
        down_spread[0].wait_recv()

    new_down = fresh[0:64]
    nothing = jnp.zeros_like(new_down)
    first = jnp.concatenate([new_down, nothing], axis=0)
    second = jnp.concatenate([nothing, new_down], axis=0)
    tz[0] = lax.dot_general(
        ctx_v[0:16], first, NT, preferred_element_type=F32
    ) + lax.dot_general(ctx_v[16:32], second, NT, preferred_element_type=F32)
    start(low_z, decoded)

    @pl.when(learner)
    def _():
        arrive(gu_xy)
        for d, copy in zip(line, gu_z):
            zz = z_to(d)
            su[zz] = summed(gu[y, x, zz], ru, (zz,)).astype(BF16)
            start([copy], learnt)
        su[z] = summed(gu[y, x, z], ru, (z,)).astype(BF16)

    arrive(base_z)
    local[4].wait()
    even, odd = halves(res_v[0:16].astype(F32), res_v[16:32].astype(F32))
    frozen = summed(sb[z], qb) + jnp.where(y == 0, even, odd)
    arrive(low_z)
    txy[0] = jnp.sum(tz[...], axis=0)
    start(low_xy, decoded)

    @pl.when(learner)
    def _():
        arrive(gu_z)
        fresh[64:96] = (packed - rates[1] * (SCALE * summed(su[z], qu))).astype(BF16)
        start(up_spread, learnt)

    @pl.when(jnp.logical_not(learner))
    def _():
        up_spread[0].wait_recv()

    new_up = fresh[64:96].astype(F32)
    turned = pltpu.roll(new_up, 64, 1)
    keep = left_half(new_up.shape)
    square = jnp.concatenate(
        [
            jnp.where(keep, new_up, 0.0),
            jnp.where(keep, turned, 0.0),
            jnp.where(keep, 0.0, turned),
            jnp.where(keep, 0.0, new_up),
        ],
        axis=0,
    ).astype(BF16)
    arrive(low_xy)
    lowered_rows = jnp.sum(txy[...], axis=0).astype(BF16)
    delta = jnp.dot(lowered_rows, square, preferred_element_type=F32)
    outs[y, x, z] = (frozen + SCALE * delta).astype(BF16)
    start(out_z, decoded)
    new_ref[...] = fresh[...]
    arrive(out_z)
    start(out_xy, decoded)
    arrive(out_xy)

    def unpack(xx, _):
        for zz in range(nz):
            column = pl.multiple_of((xx * nz + zz) * 128, 128)
            top, low = halves(outs[0, xx, zz].astype(F32), outs[1, xx, zz].astype(F32))
            dec_ref[0:16, pl.ds(column, 128)] = top.astype(BF16)
            dec_ref[16:32, pl.ds(column, 128)] = low.astype(BF16)
        return 0

    lax.fori_loop(0, nx, unpack, 0)

    sent(decoded)

    @pl.when(learner)
    def _():
        sent(learnt)


def per_device(
    sizes, rates,
    learner_inputs, learner_cotangent, down_factor, up_factor, weight, context, residual
):
    nx, nz, ny, groups = sizes
    tokens, width = learner_inputs.shape[1:]
    features = learner_cotangent.shape[2]
    rows = context.shape[1] * context.shape[2]
    xy = nx * ny - 1
    copies = 7 * (nz - 1) + (6 + nz) * xy + 2 * (groups - 1)
    blocks = (ny, nx, nz)
    scratch = [
        pltpu.VMEM((tokens, width), BF16),
        pltpu.VMEM((tokens, features), BF16),
        pltpu.VMEM(down_factor.shape[::-1], F32),
        pltpu.VMEM(up_factor.shape, F32),
        pltpu.VMEM(weight.shape, BF16),
        pltpu.VMEM((rows, 128), BF16),
        pltpu.VMEM((rows, 128), BF16),
        pltpu.VMEM((*blocks, 32, 128), BF16),
        pltpu.VMEM((*blocks, 64, 128), BF16),
        pltpu.VMEM((RANK, features), BF16),
        pltpu.VMEM((RANK, width), BF16),
    ]
    for height in (64, 32, 16):
        scratch += [
            pltpu.VMEM((*blocks, height, 128), BF16),
            pltpu.VMEM((xy, nz, height, 128), BF16),
            pltpu.VMEM((nz, height, 128), BF16),
            pltpu.VMEM((nz - 1, height, 128), BF16),
        ]
    scratch += [
        pltpu.VMEM((96, 128), BF16),
        pltpu.VMEM((nz, 16, 128), F32),
        pltpu.VMEM((xy + 1, 16, 128), F32),
        pltpu.VMEM((*blocks, 16, 128), BF16),
        pltpu.SemaphoreType.DMA((7,)),
        pltpu.SemaphoreType.DMA((copies,)),
        pltpu.SemaphoreType.DMA((copies,)),
    ]
    fresh, decoded = pl.pallas_call(
        functools.partial(kernel, sizes, rates),
        out_shape=(
            jax.ShapeDtypeStruct((96, 128), BF16),
            jax.ShapeDtypeStruct((rows, features), BF16),
        ),
        in_specs=[pl.BlockSpec(memory_space=pltpu.HBM)] * 7,
        out_specs=(pl.BlockSpec(memory_space=pltpu.VMEM),) * 2,
        scratch_shapes=scratch,
        compiler_params=pltpu.CompilerParams(
            collective_id=0, has_side_effects=True, vmem_limit_bytes=63 * 1024 * 1024
        ),
        name="lora_step",
    )(
        learner_inputs[0], learner_cotangent[0], down_factor.T, up_factor, weight,
        context[0].reshape(rows, -1), residual[0].reshape(rows, features),
    )
    new_down = fresh[0:64].T
    new_up = jnp.concatenate([fresh[64:96, 0:64], fresh[64:96, 64:128]], axis=0).T
    return new_down, new_up, decoded.reshape(residual.shape)


def solution(mesh):
    groups, shards = mesh.shape["group"], mesh.shape["shard"]
    nx, nz, ny = torus(shards)
    placed = (
        P("group", "shard", None),
        P("group", "shard", None),
        P("shard", None),
        P("shard", None),
        P("shard", None),
        P("group", None, None, "shard"),
        P("group", None, None, None),
    )

    def whole(learner_inputs, learner_cotangent, *others):
        tokens, width = learner_inputs.shape[1:]
        features = learner_cotangent.shape[2]
        rates = (
            0.5 * math.sqrt(RANK) / (SCALE * math.sqrt(width * features) * math.sqrt(tokens)),
            0.5 / (SCALE * math.sqrt(RANK) * math.sqrt(tokens)),
        )
        return jax.shard_map(
            functools.partial(per_device, (nx, nz, ny, groups), rates),
            mesh=mesh,
            in_specs=placed,
            out_specs=(P("shard", None), P("shard", None), P("group", None, None, None)),
            check_vma=False,
        )(learner_inputs, learner_cotangent, *others)

    return whole
```

time: 94.5 us -> 73.5 us (0.78)
  Pallas kernels: 83.9 us -> 67.8 us
  local copies, waits for them, and re-layouts: 9.37 us -> 4.54 us
    pallas_call x1, Pallas kernels: 83.9 us -> 67.8 us  [per_device(): pl.pallas_call(functools.partial(kernel, sizes, rates), out_shape=(jax.Sh...]
    unnamed x15 -> x2, local copies, waits for them, and re-layouts: 8.69 us -> 2.37 us
where the time goes in v2:
time: 73.5 us; the launch traced here: 72.9 us
  Pallas kernels  67.8 us (92%)
  local copies, waits for them, and re-layouts  4.54 us (6%)
    pallas_call x1, Pallas kernels, per_device(): pl.pallas_call(functools.partial(kernel, sizes, rates), out_shape=(jax.Sh...  67.8 us
    unnamed x2, local copies, waits for them, and re-layouts  2.37 us

profile of v2, /device:TPU:56, one launch (start us, length us, event | category | flops | bytes accessed | tf_op | source)
XLA Modules:
  0.0 72.9 jit_solution(8697076279045875653)
XLA Ops:
  0.6 67.8 %lora_step.1 = (bf16[96,128]{1,0:T(8,128)(2,1)}, bf16[32,4096]{1,0:T(8,128)(2,1)}) custom-call(bf16[128,8192]{1,0:T(8,128)(2,1)} %bitcast.10, bf16[128,4096]{1,0:T(8,128)(2,1)} %bitcast.11, f32[64,128]{1,0:T(8,128)} %bitcast.14, f32[64,64]{1,0:T(8,128)} %up_hbm.1, bf16[128,4096]{1,0:T(8,128)(2,1)} %w_hbm.1, bf16[32,128]{1,0:T(8,128)(2,1)} %bitcast.15, ...), custom_call_target="tpu_custom_call" | custom-call | tf_op jit(solution)/shard_map/lora_step/pallas_call | solution.py:416
  68.4 1.3 %slice_bitcast_fusion = bf16[128,64]{0,1:T(8,128)(2,1)} fusion(bf16[96,128]{1,0:T(8,128)(2,1)} %get-tuple-element.5), kind=kLoop, calls=%fused_computation.1 | loop fusion | bytes 32768 | tf_op jit(solution)/shard_map/transpose | solution.py:433
  69.7 0.8 %fusion = (bf16[32,64]{1,0:T(8,128)(2,1)S(1)}, bf16[32,64]{1,0:T(8,128)(2,1)S(1)}) fusion(bf16[96,128]{1,0:T(8,128)(2,1)} %get-tuple-element.5), kind=kLoop, calls=%fused_computation.2 | loop fusion | bytes 16384 | tf_op jit(solution)/shard_map/slice | solution.py:434
  70.6 0.7 copy.10
  71.3 1.7 %copy.12 = bf16[1,4,8,4096]{3,2,1,0:T(8,128)(2,1)} copy(bf16[1,4,8,4096]{3,2,1,0:T(8,128)(2,1)} %bitcast.13) | data formatting | bytes 524288
  (1 shorter events, 0.0 us)

commit v3 on v2

--- a/solution.py
+++ b/solution.py
@@ -33,7 +33,7 @@
 def kernel(
     sizes, rates,
     x_hbm, c_hbm, down_hbm, up_hbm, w_hbm, ctx_hbm, res_hbm,
-    new_ref, dec_ref,
+    new_ref, out_hbm,
     x_v, c_v, down_v, up_v, w_v, ctx_v, res_v,
     up_all, down_all, up_flat, down_flat,
     gd, rd, sd, qd, gu, ru, su, qu,
@@ -48,6 +48,8 @@
     x = shard // (ny * nz)
     other = 1 - y
     learner = group == 0
+    helper_group = jnp.where(other == 1, groups - 2, 2)
+    helper = group == jnp.where(y == 1, groups - 2, 2)
 
     def at(xx, zz, yy):
         return (xx * nz + zz) * ny + yy
@@ -103,6 +105,14 @@
             barrier, inc=1, device_id={"group": 0}, device_id_type=pl.DeviceIdType.MESH
         )
 
+    @pl.when(learner)
+    def _():
+        for d in range(nx):
+            pl.semaphore_signal(
+                barrier, inc=1, device_id={"group": helper_group, "shard": at(x_to(d), z, other)},
+                device_id_type=pl.DeviceIdType.MESH,
+            )
+
     used = [0]
 
     def remote(src, dst, peer):
@@ -122,6 +132,23 @@
             for i, (dx, dy) in enumerate(plane)
         ]
 
+    def beside(ref):
+        return [remote(ref, ref, at(x_to(d), z, y)) for d in rows if d]
+
+    def helped(ref):
+        copies = []
+        for d in rows:
+            k = used[0]
+            used[0] += 1
+            copies.append(
+                pltpu.make_async_remote_copy(
+                    src_ref=ref, dst_ref=ref, send_sem=send_sem.at[k], recv_sem=recv_sem.at[k],
+                    device_id={"group": 0, "shard": at(x_to(d), z, other)},
+                    device_id_type=pl.DeviceIdType.MESH,
+                )
+            )
+        return copies
+
     def start(copies, started):
         for copy in copies:
             copy.start()
@@ -135,15 +162,14 @@
         for copy in started:
             copy.wait_send()
 
-    learnt, decoded = [], []
+    learnt, lent, decoded = [], [], []
 
     up_z = along(lambda zz: up_all.at[y, x, z], lambda i, d: up_all.at[y, x, z])
-    up_xy = [
-        across(lambda xx, yy: up_all.at[y, x, zz], lambda i: up_all.at[y, x, zz])
-        for zz in [z] + [lax.rem(z + nz - d, nz) for d in line[::-1]]
-    ]
     down_z = along(lambda zz: down_all.at[y, x, z], lambda i, d: down_all.at[y, x, z])
-    down_xy = across(lambda xx, yy: down_all.at[y, x], lambda i: down_all.at[y, x])
+    up_x = beside(up_all.at[y, x])
+    up_y = helped(up_all.at[y, x])
+    down_x = beside(down_all.at[y, x])
+    down_y = helped(down_all.at[y, x])
     gd_xy = across(lambda xx, yy: gd.at[yy, xx], lambda i: rd.at[i])
     gd_z = along(lambda zz: sd.at[zz], lambda i, d: qd.at[i])
     gu_xy = across(lambda xx, yy: gu.at[yy, xx], lambda i: ru.at[i])
@@ -153,7 +179,8 @@
     low_z = along(lambda zz: tz.at[0], lambda i, d: tz.at[i + 1])
     low_xy = across(lambda xx, yy: txy.at[0], lambda i: txy.at[i + 1])
     out_z = along(lambda zz: outs.at[y, x, z], lambda i, d: outs.at[y, x, z])
-    out_xy = across(lambda xx, yy: outs.at[y, x], lambda i: outs.at[y, x])
+    out_xy = across(lambda xx, yy: outs.at[y, x], lambda i: out_hbm.at[y, x])
+    out_own = pltpu.make_async_copy(outs.at[y, x], out_hbm.at[y, x], local_sem.at[7])
 
     def spread(part, k):
         order = [g for hi in (2, 1, 3, 0) for g in (2 * hi, 2 * hi + 1) if 0 < g < groups]
@@ -198,24 +225,43 @@
 
     local[0].wait()
     packed = packed_up()
-    pl.semaphore_wait(barrier, len(peers) + jnp.where(learner, groups - 1, 0))
-
-    @pl.when(learner)
+    pl.semaphore_wait(
+        barrier,
+        len(peers) + jnp.where(learner, groups - 1, 0) + jnp.where(helper, nx, 0),
+    )
+
+    local[1].wait()
+
+    @pl.when(jnp.logical_or(learner, helper))
     def _():
         up_all[y, x, z] = packed.astype(BF16)
-        start(up_z, learnt)
-        start(up_xy[0], learnt)
-        local[1].wait()
+        for copy in up_z:
+            copy.start()
         down_all[y, x, z] = down_v[...].astype(BF16)
-        for copy, onward in zip(up_z[::-1], up_xy[1:]):
-            arrive([copy])
-            start(onward, learnt)
-        start(down_z, learnt)
-
-    @pl.when(jnp.logical_not(learner))
-    def _():
-        local[1].wait()
-
+        for copy in down_z:
+            copy.start()
+        arrive(up_z)
+
+        @pl.when(learner)
+        def _():
+            start(up_x, learnt)
+
+        @pl.when(helper)
+        def _():
+            start(up_y, lent)
+
+        arrive(down_z)
+
+        @pl.when(learner)
+        def _():
+            start(down_x, learnt)
+
+        @pl.when(helper)
+        def _():
+            start(down_y, lent)
+
+    learnt.extend(up_z + down_z)
+    lent.extend(up_z + down_z)
     local[2].wait()
     local[3].wait()
     lax.fori_loop(0, nx, project, 0)
@@ -227,11 +273,9 @@
 
     @pl.when(learner)
     def _():
-        arrive(down_z)
-        start(down_xy, learnt)
         local[5].wait()
-        for copies in up_xy:
-            arrive(copies)
+        arrive(up_x)
+        arrive(up_y)
 
         def unpack_up(xx, _):
             for zz in range(nz):
@@ -257,7 +301,8 @@
                 gd[1, xx, zz] = block[:, 128:256]
             start([c for c, p in zip(gd_xy, plane) if p[0] == dx], learnt)
         start(base_xy, [])
-        arrive(down_xy)
+        arrive(down_x)
+        arrive(down_y)
 
         def flatten(xx, _):
             for zz in range(nz):
@@ -354,23 +399,33 @@
     new_ref[...] = fresh[...]
     arrive(out_z)
     start(out_xy, decoded)
+    out_own.start()
     arrive(out_xy)
 
-    def unpack(xx, _):
+    out_own.wait()
+    sent(decoded)
+
+    @pl.when(learner)
+    def _():
+        sent(learnt)
+
+    @pl.when(helper)
+    def _():
+        sent(lent)
+
+
+def finish(fresh_ref, outs_ref, down_ref, up_ref, dec_ref):
+    ny, nx, nz = outs_ref.shape[:3]
+    down_ref[...] = fresh_ref[0:64]
+    packed = fresh_ref[64:96].astype(F32)
+    up_t = jnp.concatenate([packed, pltpu.roll(packed, 64, 1)], axis=0)
+    up_ref[...] = up_t.T[0:64].astype(BF16)
+    for xx in range(nx):
         for zz in range(nz):
-            column = pl.multiple_of((xx * nz + zz) * 128, 128)
-            top, low = halves(outs[0, xx, zz].astype(F32), outs[1, xx, zz].astype(F32))
-            dec_ref[0:16, pl.ds(column, 128)] = top.astype(BF16)
-            dec_ref[16:32, pl.ds(column, 128)] = low.astype(BF16)
-        return 0
-
-    lax.fori_loop(0, nx, unpack, 0)
-
-    sent(decoded)
-
-    @pl.when(learner)
-    def _():
-        sent(learnt)
+            column = (xx * nz + zz) * 128
+            top, low = halves(outs_ref[0, xx, zz].astype(F32), outs_ref[1, xx, zz].astype(F32))
+            dec_ref[0:16, column : column + 128] = top.astype(BF16)
+            dec_ref[16:32, column : column + 128] = low.astype(BF16)
 
 
 def per_device(
@@ -382,7 +437,7 @@
     features = learner_cotangent.shape[2]
     rows = context.shape[1] * context.shape[2]
     xy = nx * ny - 1
-    copies = 7 * (nz - 1) + (6 + nz) * xy + 2 * (groups - 1)
+    copies = 7 * (nz - 1) + 5 * xy + 2 * (2 * nx - 1) + 2 * (groups - 1)
     blocks = (ny, nx, nz)
     scratch = [
         pltpu.VMEM((tokens, width), BF16),
@@ -409,18 +464,21 @@
         pltpu.VMEM((nz, 16, 128), F32),
         pltpu.VMEM((xy + 1, 16, 128), F32),
         pltpu.VMEM((*blocks, 16, 128), BF16),
-        pltpu.SemaphoreType.DMA((7,)),
+        pltpu.SemaphoreType.DMA((8,)),
         pltpu.SemaphoreType.DMA((copies,)),
         pltpu.SemaphoreType.DMA((copies,)),
     ]
-    fresh, decoded = pl.pallas_call(
+    fresh, outs = pl.pallas_call(
         functools.partial(kernel, sizes, rates),
         out_shape=(
             jax.ShapeDtypeStruct((96, 128), BF16),
-            jax.ShapeDtypeStruct((rows, features), BF16),
+            jax.ShapeDtypeStruct((*blocks, 16, 128), BF16),
         ),
         in_specs=[pl.BlockSpec(memory_space=pltpu.HBM)] * 7,
-        out_specs=(pl.BlockSpec(memory_space=pltpu.VMEM),) * 2,
+        out_specs=(
+            pl.BlockSpec(memory_space=pltpu.VMEM),
+            pl.BlockSpec(memory_space=pltpu.HBM),
+        ),
         scratch_shapes=scratch,
         compiler_params=pltpu.CompilerParams(
             collective_id=0, has_side_effects=True, vmem_limit_bytes=63 * 1024 * 1024
@@ -430,9 +488,19 @@
         learner_inputs[0], learner_cotangent[0], down_factor.T, up_factor, weight,
         context[0].reshape(rows, -1), residual[0].reshape(rows, features),
     )
-    new_down = fresh[0:64].T
-    new_up = jnp.concatenate([fresh[64:96, 0:64], fresh[64:96, 64:128]], axis=0).T
-    return new_down, new_up, decoded.reshape(residual.shape)
+    new_down, new_up, decoded = pl.pallas_call(
+        finish,
+        out_shape=(
+            jax.ShapeDtypeStruct((64, 128), BF16),
+            jax.ShapeDtypeStruct((64, 64), BF16),
+            jax.ShapeDtypeStruct((rows, features), BF16),
+        ),
+        in_specs=[pl.BlockSpec(memory_space=pltpu.VMEM)] * 2,
+        out_specs=(pl.BlockSpec(memory_space=pltpu.VMEM),) * 3,
+        compiler_params=pltpu.CompilerParams(vmem_limit_bytes=63 * 1024 * 1024),
+        name="finish",
+    )(fresh, outs)
+    return new_down.T, new_up, decoded.reshape(residual.shape)
 
 
 def solution(mesh):

time: 73.5 us -> 68.5 us (0.932)
  local copies, waits for them, and re-layouts: 4.54 us -> 0 us
    unnamed x2 -> x0, local copies, waits for them, and re-layouts: 2.37 us -> none
    pallas_call x1, Pallas kernels: 67.8 us -> 65.6 us  [per_device(): pl.pallas_call(functools.partial(kernel, sizes, rates), out_shape=(jax.Sh...]
    pallas_call x0 -> x1, Pallas kernels: none -> 1.85 us  [per_device(): pl.pallas_call(finish, out_shape=(jax.ShapeDtypeStruct((64, 128), BF16),...]
    transpose x1 -> x0, local copies, waits for them, and re-layouts: 1.32 us -> none  [per_device(): new_down = fresh[0:64].T]
    slice x1 -> x0, local copies, waits for them, and re-layouts: 0.85 us -> none  [per_device(): fresh[64:96, 0:64]]
where the time goes in v3:
time: 68.5 us; the launch traced here: 68.1 us
  Pallas kernels  67.4 us (98%)
    pallas_call x1, Pallas kernels, per_device(): pl.pallas_call(functools.partial(kernel, sizes, rates), out_shape=(jax.Sh...  65.6 us
    pallas_call x1, Pallas kernels, per_device(): pl.pallas_call(finish, out_shape=(jax.ShapeDtypeStruct((64, 128), BF16),...  1.85 us

profile of v3, /device:TPU:56, one launch (start us, length us, event | category | flops | bytes accessed | tf_op | source)
XLA Modules:
  0.0 68.1 jit_solution(11396074059321561746)
XLA Ops:
  0.6 65.6 %lora_step.1 = (bf16[96,128]{1,0:T(8,128)(2,1)}, bf16[2,4,8,16,128]{4,3,2,1,0:T(8,128)(2,1)}) custom-call(bf16[128,8192]{1,0:T(8,128)(2,1)} %bitcast.7, bf16[128,4096]{1,0:T(8,128)(2,1)} %bitcast.8, f32[64,128]{1,0:T(8,128)} %bitcast.10, f32[64,64]{1,0:T(8,128)} %up_hbm.1, bf16[128,4096]{1,0:T(8,128)(2,1)} %w_hbm.1, bf16[32,128]{1,0:T(8,128)(2,1)} %bitcast.11, ...), custom_call_target="tpu_custom_call" | custom-call | tf_op jit(solution)/shard_map/lora_step/pallas_call | solution.py:471
  66.2 1.9 %finish.1 = (bf16[64,128]{1,0:T(8,128)(2,1)}, bf16[64,64]{1,0:T(8,128)(2,1)}, bf16[32,4096]{1,0:T(8,128)(2,1)}) custom-call(bf16[96,128]{1,0:T(8,128)(2,1)} %get-tuple-element.8.fresh_ref, bf16[2,4,8,16,128]{4,3,2,1,0:T(8,128)(2,1)} %get-tuple-element.9.outs_ref), custom_call_target="tpu_custom_call" | custom-call | tf_op jit(solution)/shard_map/finish/pallas_call | solution.py:491

commit v4 on v3

--- a/solution.py
+++ b/solution.py
@@ -38,6 +38,7 @@
     up_all, down_all, up_flat, down_flat,
     gd, rd, sd, qd, gu, ru, su, qu,
     base, rb, sb, qb, fresh, tz, txy, outs,
+    base_line, up_line, frozen, squares,
     local_sem, send_sem, recv_sem,
 ):
     nx, nz, ny, groups = sizes
@@ -78,20 +79,12 @@
                 (down_hbm, down_v),
                 (ctx_hbm, ctx_v),
                 (w_hbm, w_v),
-                (res_hbm.at[:, pl.ds(pl.multiple_of((shard // ny) * 128, 128), 128)], res_v),
+                (res_hbm.at[:, pl.ds(pl.multiple_of(x * (nz * 128), 128), nz * 128)], res_v),
                 (c_hbm, c_v),
                 (x_hbm, x_v),
             ]
         )
     ]
-    for copy in local[:5]:
-        copy.start()
-
-    @pl.when(learner)
-    def _():
-        local[5].start()
-        local[6].start()
-
     barrier = pltpu.get_barrier_semaphore()
     peers = [at(x, z_to(d), y) for d in line] + [at(x_to(dx), z, y_to(dy)) for dx, dy in plane]
     for peer in peers:
@@ -112,6 +105,14 @@
                 barrier, inc=1, device_id={"group": helper_group, "shard": at(x_to(d), z, other)},
                 device_id_type=pl.DeviceIdType.MESH,
             )
+
+    for copy in local[:5]:
+        copy.start()
+
+    @pl.when(learner)
+    def _():
+        local[5].start()
+        local[6].start()
 
     used = [0]
 
@@ -176,11 +177,12 @@
     gu_z = along(lambda zz: su.at[zz], lambda i, d: qu.at[i])
     base_xy = across(lambda xx, yy: base.at[yy, xx], lambda i: rb.at[i])
     base_z = along(lambda zz: sb.at[zz], lambda i, d: qb.at[i])
+    base_g = along(lambda zz: base_line.at[z], lambda i, d: base_line.at[z])
+    up_g = along(lambda zz: up_line.at[z], lambda i, d: up_line.at[z])
     low_z = along(lambda zz: tz.at[0], lambda i, d: tz.at[i + 1])
     low_xy = across(lambda xx, yy: txy.at[0], lambda i: txy.at[i + 1])
-    out_z = along(lambda zz: outs.at[y, x, z], lambda i, d: outs.at[y, x, z])
-    out_xy = across(lambda xx, yy: outs.at[y, x], lambda i: out_hbm.at[y, x])
-    out_own = pltpu.make_async_copy(outs.at[y, x], out_hbm.at[y, x], local_sem.at[7])
+    out_xy = across(lambda xx, yy: outs, lambda i: out_hbm.at[y, x])
+    out_own = pltpu.make_async_copy(outs, out_hbm.at[y, x], local_sem.at[7])
 
     def spread(part, k):
         order = [g for hi in (2, 1, 3, 0) for g in (2 * hi, 2 * hi + 1) if 0 < g < groups]
@@ -192,8 +194,8 @@
             for i, g in enumerate(order)
         ]
 
-    down_spread = spread(fresh.at[0:64], used[0])
-    up_spread = spread(fresh.at[64:96], used[0] + groups - 1)
+    down_spread = spread(fresh, used[0])
+    up_spread = spread(up_line.at[z], used[0] + groups - 1)
 
     def summed(own, others, index=()):
         total = own.astype(F32)
@@ -223,6 +225,21 @@
             copy.start()
         sb[z] = summed(base[y, x, z], rb, (z,)).astype(BF16)
 
+    def base_total():
+        arrive(base_z)
+        base_line[z] = summed(sb[z], qb).astype(BF16)
+        start(base_g, [])
+
+    def freeze():
+        arrive(base_g)
+        local[4].wait()
+        for zz in range(nz):
+            held = res_v[:, zz * 128 : (zz + 1) * 128].astype(F32)
+            even, odd = halves(held[0:16], held[16:32])
+            frozen[:, zz * 128 : (zz + 1) * 128] = base_line[zz].astype(F32) + jnp.where(
+                y == 0, even, odd
+            )
+
     local[0].wait()
     packed = packed_up()
     pl.semaphore_wait(
@@ -270,6 +287,8 @@
     def _():
         start(base_xy, [])
         base_lines()
+        base_total()
+        freeze()
 
     @pl.when(learner)
     def _():
@@ -334,16 +353,22 @@
         base_lines()
         arrive(gd_z)
         total = summed(sd[z], qd)
-        fresh[0:64] = (down_v[...] - rates[0] * (SCALE * total)).astype(BF16)
+        fresh[...] = (down_v[...] - rates[0] * (SCALE * total)).astype(BF16)
         start(down_spread, learnt)
-
-    decoded.extend(base_xy + base_z)
+        arrive(gu_xy)
+        for d, copy in zip(line, gu_z):
+            zz = z_to(d)
+            su[zz] = summed(gu[y, x, zz], ru, (zz,)).astype(BF16)
+            start([copy], learnt)
+        su[z] = summed(gu[y, x, z], ru, (z,)).astype(BF16)
+
+    decoded.extend(base_xy + base_z + base_g)
 
     @pl.when(jnp.logical_not(learner))
     def _():
         down_spread[0].wait_recv()
 
-    new_down = fresh[0:64]
+    new_down = fresh[...]
     nothing = jnp.zeros_like(new_down)
     first = jnp.concatenate([new_down, nothing], axis=0)
     second = jnp.concatenate([nothing, new_down], axis=0)
@@ -354,50 +379,48 @@
 
     @pl.when(learner)
     def _():
-        arrive(gu_xy)
-        for d, copy in zip(line, gu_z):
-            zz = z_to(d)
-            su[zz] = summed(gu[y, x, zz], ru, (zz,)).astype(BF16)
-            start([copy], learnt)
-        su[z] = summed(gu[y, x, z], ru, (z,)).astype(BF16)
-
-    arrive(base_z)
-    local[4].wait()
-    even, odd = halves(res_v[0:16].astype(F32), res_v[16:32].astype(F32))
-    frozen = summed(sb[z], qb) + jnp.where(y == 0, even, odd)
+        base_total()
+        arrive(gu_z)
+        up_line[z] = (packed - rates[1] * (SCALE * summed(su[z], qu))).astype(BF16)
+        start(up_spread, learnt)
+        start(up_g, [])
+
     arrive(low_z)
     txy[0] = jnp.sum(tz[...], axis=0)
     start(low_xy, decoded)
 
     @pl.when(learner)
     def _():
-        arrive(gu_z)
-        fresh[64:96] = (packed - rates[1] * (SCALE * summed(su[z], qu))).astype(BF16)
-        start(up_spread, learnt)
+        freeze()
 
     @pl.when(jnp.logical_not(learner))
     def _():
         up_spread[0].wait_recv()
-
-    new_up = fresh[64:96].astype(F32)
-    turned = pltpu.roll(new_up, 64, 1)
-    keep = left_half(new_up.shape)
-    square = jnp.concatenate(
-        [
-            jnp.where(keep, new_up, 0.0),
-            jnp.where(keep, turned, 0.0),
-            jnp.where(keep, 0.0, turned),
-            jnp.where(keep, 0.0, new_up),
-        ],
-        axis=0,
-    ).astype(BF16)
+        start(up_g, [])
+
+    decoded.extend(up_g)
+    new_ref[0:64] = fresh[...]
+    new_ref[64:96] = up_line[z]
+    arrive(up_g)
+    for zz in range(nz):
+        new_up = up_line[zz].astype(F32)
+        turned = pltpu.roll(new_up, 64, 1)
+        keep = left_half(new_up.shape)
+        squares[:, zz * 128 : (zz + 1) * 128] = jnp.concatenate(
+            [
+                jnp.where(keep, new_up, 0.0),
+                jnp.where(keep, turned, 0.0),
+                jnp.where(keep, 0.0, turned),
+                jnp.where(keep, 0.0, new_up),
+            ],
+            axis=0,
+        ).astype(BF16)
     arrive(low_xy)
     lowered_rows = jnp.sum(txy[...], axis=0).astype(BF16)
-    delta = jnp.dot(lowered_rows, square, preferred_element_type=F32)
-    outs[y, x, z] = (frozen + SCALE * delta).astype(BF16)
-    start(out_z, decoded)
-    new_ref[...] = fresh[...]
-    arrive(out_z)
+    delta = jnp.dot(lowered_rows, squares[...], preferred_element_type=F32)
+    for zz in range(nz):
+        part = slice(zz * 128, (zz + 1) * 128)
+        outs[zz] = (frozen[:, part] + SCALE * delta[:, part]).astype(BF16)
     start(out_xy, decoded)
     out_own.start()
     arrive(out_xy)
@@ -437,7 +460,7 @@
     features = learner_cotangent.shape[2]
     rows = context.shape[1] * context.shape[2]
     xy = nx * ny - 1
-    copies = 7 * (nz - 1) + 5 * xy + 2 * (2 * nx - 1) + 2 * (groups - 1)
+    copies = 8 * (nz - 1) + 5 * xy + 2 * (2 * nx - 1) + 2 * (groups - 1)
     blocks = (ny, nx, nz)
     scratch = [
         pltpu.VMEM((tokens, width), BF16),
@@ -446,7 +469,7 @@
         pltpu.VMEM(up_factor.shape, F32),
         pltpu.VMEM(weight.shape, BF16),
         pltpu.VMEM((rows, 128), BF16),
-        pltpu.VMEM((rows, 128), BF16),
+        pltpu.VMEM((rows, nz * 128), BF16),
         pltpu.VMEM((*blocks, 32, 128), BF16),
         pltpu.VMEM((*blocks, 64, 128), BF16),
         pltpu.VMEM((RANK, features), BF16),
@@ -460,10 +483,14 @@
             pltpu.VMEM((nz - 1, height, 128), BF16),
         ]
     scratch += [
-        pltpu.VMEM((96, 128), BF16),
+        pltpu.VMEM((64, 128), BF16),
         pltpu.VMEM((nz, 16, 128), F32),
         pltpu.VMEM((xy + 1, 16, 128), F32),
-        pltpu.VMEM((*blocks, 16, 128), BF16),
+        pltpu.VMEM((nz, 16, 128), BF16),
+        pltpu.VMEM((nz, 16, 128), BF16),
+        pltpu.VMEM((nz, 32, 128), BF16),
+        pltpu.VMEM((16, nz * 128), F32),
+        pltpu.VMEM((128, nz * 128), BF16),
         pltpu.SemaphoreType.DMA((8,)),
         pltpu.SemaphoreType.DMA((copies,)),
         pltpu.SemaphoreType.DMA((copies,)),

time: 68.5 us -> 65 us (0.949)
  Pallas kernels: 67.4 us -> 63.7 us
    pallas_call x1, Pallas kernels: 65.6 us -> 61.8 us  [per_device(): pl.pallas_call(functools.partial(kernel, sizes, rates), out_shape=(jax.Sh...]
where the time goes in v4:
time: 65 us; the launch traced here: 64.3 us
  Pallas kernels  63.7 us (98%)
    pallas_call x1, Pallas kernels, per_device(): pl.pallas_call(functools.partial(kernel, sizes, rates), out_shape=(jax.Sh...  61.8 us
    pallas_call x1, Pallas kernels, per_device(): pl.pallas_call(finish, out_shape=(jax.ShapeDtypeStruct((64, 128), BF16),...  1.85 us

profile of v4, /device:TPU:56, one launch (start us, length us, event | category | flops | bytes accessed | tf_op | source)
XLA Modules:
  0.0 64.3 jit_solution(4901300098424141272)
XLA Ops:
  0.6 61.8 %lora_step.1 = (bf16[96,128]{1,0:T(8,128)(2,1)}, bf16[2,4,8,16,128]{4,3,2,1,0:T(8,128)(2,1)}) custom-call(bf16[128,8192]{1,0:T(8,128)(2,1)} %bitcast.7, bf16[128,4096]{1,0:T(8,128)(2,1)} %bitcast.8, f32[64,128]{1,0:T(8,128)} %bitcast.10, f32[64,64]{1,0:T(8,128)} %up_hbm.1, bf16[128,4096]{1,0:T(8,128)(2,1)} %w_hbm.1, bf16[32,128]{1,0:T(8,128)(2,1)} %bitcast.11, ...), custom_call_target="tpu_custom_call" | custom-call | tf_op jit(solution)/shard_map/lora_step/pallas_call | solution.py:498
  62.5 1.9 %finish.1 = (bf16[64,128]{1,0:T(8,128)(2,1)}, bf16[64,64]{1,0:T(8,128)(2,1)}, bf16[32,4096]{1,0:T(8,128)(2,1)}) custom-call(bf16[96,128]{1,0:T(8,128)(2,1)} %get-tuple-element.8.fresh_ref, bf16[2,4,8,16,128]{4,3,2,1,0:T(8,128)(2,1)} %get-tuple-element.9.outs_ref), custom_call_target="tpu_custom_call" | custom-call | tf_op jit(solution)/shard_map/finish/pallas_call | solution.py:518

commit v5 on v4

--- a/solution.py
+++ b/solution.py
@@ -33,13 +33,13 @@
 def kernel(
     sizes, rates,
     x_hbm, c_hbm, down_hbm, up_hbm, w_hbm, ctx_hbm, res_hbm,
-    new_ref, out_hbm,
+    new_hbm, out_hbm,
     x_v, c_v, down_v, up_v, w_v, ctx_v, res_v,
     up_all, down_all, up_flat, down_flat,
     gd, rd, sd, qd, gu, ru, su, qu,
     base, rb, sb, qb, fresh, tz, txy, outs,
     base_line, up_line, frozen, squares,
-    local_sem, send_sem, recv_sem,
+    local_sem, send_sem, recv_sem, ready_sem,
 ):
     nx, nz, ny, groups = sizes
     group = lax.axis_index("group")
@@ -92,18 +92,16 @@
             barrier, inc=1, device_id={"shard": peer}, device_id_type=pl.DeviceIdType.MESH
         )
 
-    @pl.when(jnp.logical_not(learner))
-    def _():
-        pl.semaphore_signal(
-            barrier, inc=1, device_id={"group": 0}, device_id_type=pl.DeviceIdType.MESH
-        )
-
     @pl.when(learner)
     def _():
         for d in range(nx):
             pl.semaphore_signal(
                 barrier, inc=1, device_id={"group": helper_group, "shard": at(x_to(d), z, other)},
                 device_id_type=pl.DeviceIdType.MESH,
+            )
+        for g in range(1, groups):
+            pl.semaphore_signal(
+                barrier, inc=1, device_id={"group": g}, device_id_type=pl.DeviceIdType.MESH
             )
 
     for copy in local[:5]:
@@ -244,8 +242,14 @@
     packed = packed_up()
     pl.semaphore_wait(
         barrier,
-        len(peers) + jnp.where(learner, groups - 1, 0) + jnp.where(helper, nx, 0),
+        len(peers) + jnp.where(learner, 0, 1) + jnp.where(helper, nx, 0),
     )
+
+    @pl.when(jnp.logical_not(learner))
+    def _():
+        pl.semaphore_signal(
+            ready_sem, inc=1, device_id={"group": 0}, device_id_type=pl.DeviceIdType.MESH
+        )
 
     local[1].wait()
 
@@ -354,6 +358,7 @@
         arrive(gd_z)
         total = summed(sd[z], qd)
         fresh[...] = (down_v[...] - rates[0] * (SCALE * total)).astype(BF16)
+        pl.semaphore_wait(ready_sem, groups - 1)
         start(down_spread, learnt)
         arrive(gu_xy)
         for d, copy in zip(line, gu_z):
@@ -398,9 +403,22 @@
         up_spread[0].wait_recv()
         start(up_g, [])
 
-    decoded.extend(up_g)
-    new_ref[0:64] = fresh[...]
-    new_ref[64:96] = up_line[z]
+    written = [
+        pltpu.make_async_copy(fresh, new_hbm.at[0:64], local_sem.at[8]),
+        pltpu.make_async_copy(up_line.at[z], new_hbm.at[64:96], local_sem.at[9]),
+    ]
+    for copy in written:
+        copy.start()
+    sent([copy for copy in decoded if not any(copy is late for late in low_xy)])
+
+    @pl.when(learner)
+    def _():
+        sent(learnt)
+
+    @pl.when(helper)
+    def _():
+        sent(lent)
+
     arrive(up_g)
     for zz in range(nz):
         new_up = up_line[zz].astype(F32)
@@ -426,15 +444,9 @@
     arrive(out_xy)
 
     out_own.wait()
-    sent(decoded)
-
-    @pl.when(learner)
-    def _():
-        sent(learnt)
-
-    @pl.when(helper)
-    def _():
-        sent(lent)
+    for copy in written:
+        copy.wait()
+    sent(up_g + low_xy + out_xy)
 
 
 def finish(fresh_ref, outs_ref, down_ref, up_ref, dec_ref):
@@ -491,9 +503,10 @@
         pltpu.VMEM((nz, 32, 128), BF16),
         pltpu.VMEM((16, nz * 128), F32),
         pltpu.VMEM((128, nz * 128), BF16),
-        pltpu.SemaphoreType.DMA((8,)),
+        pltpu.SemaphoreType.DMA((10,)),
         pltpu.SemaphoreType.DMA((copies,)),
         pltpu.SemaphoreType.DMA((copies,)),
+        pltpu.SemaphoreType.REGULAR,
     ]
     fresh, outs = pl.pallas_call(
         functools.partial(kernel, sizes, rates),
@@ -502,10 +515,7 @@
             jax.ShapeDtypeStruct((*blocks, 16, 128), BF16),
         ),
         in_specs=[pl.BlockSpec(memory_space=pltpu.HBM)] * 7,
-        out_specs=(
-            pl.BlockSpec(memory_space=pltpu.VMEM),
-            pl.BlockSpec(memory_space=pltpu.HBM),
-        ),
+        out_specs=(pl.BlockSpec(memory_space=pltpu.HBM),) * 2,
         scratch_shapes=scratch,
         compiler_params=pltpu.CompilerParams(
             collective_id=0, has_side_effects=True, vmem_limit_bytes=63 * 1024 * 1024

time: 65 us -> 61.9 us (0.952)
  Pallas kernels: 63.7 us -> 61 us
    pallas_call x1, Pallas kernels: 61.8 us -> 59.1 us  [per_device(): pl.pallas_call(functools.partial(kernel, sizes, rates), out_shape=(jax.Sh...]
where the time goes in v5:
time: 61.9 us; the launch traced here: 61.6 us
  Pallas kernels  61 us (99%)
  between operations  0.64 us (1%)
    pallas_call x1, Pallas kernels, per_device(): pl.pallas_call(functools.partial(kernel, sizes, rates), out_shape=(jax.Sh...  59.1 us
    pallas_call x1, Pallas kernels, per_device(): pl.pallas_call(finish, out_shape=(jax.ShapeDtypeStruct((64, 128), BF16),...  1.85 us

profile of v5, /device:TPU:56, one launch (start us, length us, event | category | flops | bytes accessed | tf_op | source)
XLA Modules:
  0.0 61.6 jit_solution(10893216643856312301)
XLA Ops:
  0.6 59.1 %lora_step.1 = (bf16[96,128]{1,0:T(8,128)(2,1)}, bf16[2,4,8,16,128]{4,3,2,1,0:T(8,128)(2,1)}) custom-call(bf16[128,8192]{1,0:T(8,128)(2,1)} %bitcast.7, bf16[128,4096]{1,0:T(8,128)(2,1)} %bitcast.8, f32[64,128]{1,0:T(8,128)} %bitcast.10, f32[64,64]{1,0:T(8,128)} %up_hbm.1, bf16[128,4096]{1,0:T(8,128)(2,1)} %w_hbm.1, bf16[32,128]{1,0:T(8,128)(2,1)} %bitcast.11, ...), custom_call_target="tpu_custom_call" | custom-call | tf_op jit(solution)/shard_map/lora_step/pallas_call | solution.py:511
  59.8 1.9 %finish.1 = (bf16[64,128]{1,0:T(8,128)(2,1)}, bf16[64,64]{1,0:T(8,128)(2,1)}, bf16[32,4096]{1,0:T(8,128)(2,1)}) custom-call(bf16[96,128]{1,0:T(8,128)(2,1)} %get-tuple-element.8.fresh_ref, bf16[2,4,8,16,128]{4,3,2,1,0:T(8,128)(2,1)} %get-tuple-element.9.outs_ref), custom_call_target="tpu_custom_call" | custom-call | tf_op jit(solution)/shard_map/finish/pallas_call | solution.py:528

commit v6 on v5

--- a/solution.py
+++ b/solution.py
@@ -94,7 +94,7 @@
 
     @pl.when(learner)
     def _():
-        for d in range(nx):
+        for d in range(1, nx):
             pl.semaphore_signal(
                 barrier, inc=1, device_id={"group": helper_group, "shard": at(x_to(d), z, other)},
                 device_id_type=pl.DeviceIdType.MESH,
@@ -136,7 +136,7 @@
 
     def helped(ref):
         copies = []
-        for d in rows:
+        for d in rows[:-1]:
             k = used[0]
             used[0] += 1
             copies.append(
@@ -166,8 +166,10 @@
     up_z = along(lambda zz: up_all.at[y, x, z], lambda i, d: up_all.at[y, x, z])
     down_z = along(lambda zz: down_all.at[y, x, z], lambda i, d: down_all.at[y, x, z])
     up_x = beside(up_all.at[y, x])
+    up_x += [remote(up_all.at[y, x], up_all.at[y, x], at(x, z, other))]
     up_y = helped(up_all.at[y, x])
     down_x = beside(down_all.at[y, x])
+    down_p = [remote(down_all.at[y, x], down_all.at[y, x], at(x, z, other))]
     down_y = helped(down_all.at[y, x])
     gd_xy = across(lambda xx, yy: gd.at[yy, xx], lambda i: rd.at[i])
     gd_z = along(lambda zz: sd.at[zz], lambda i, d: qd.at[i])
@@ -242,7 +244,7 @@
     packed = packed_up()
     pl.semaphore_wait(
         barrier,
-        len(peers) + jnp.where(learner, 0, 1) + jnp.where(helper, nx, 0),
+        len(peers) + jnp.where(learner, 0, 1) + jnp.where(helper, nx - 1, 0),
     )
 
     @pl.when(jnp.logical_not(learner))
@@ -275,7 +277,7 @@
 
         @pl.when(learner)
         def _():
-            start(down_x, learnt)
+            start(down_x + down_p, learnt)
 
         @pl.when(helper)
         def _():
@@ -324,18 +326,17 @@
                 gd[1, xx, zz] = block[:, 128:256]
             start([c for c, p in zip(gd_xy, plane) if p[0] == dx], learnt)
         start(base_xy, [])
+        def flatten(plane_y):
+            for xx in range(nx):
+                for zz in range(nz):
+                    column = pl.multiple_of((xx * nz + zz) * 256 + plane_y * 128, 128)
+                    down_flat[:, pl.ds(column, 128)] = down_all[plane_y, xx, zz]
+
         arrive(down_x)
+        flatten(y)
+        arrive(down_p)
         arrive(down_y)
-
-        def flatten(xx, _):
-            for zz in range(nz):
-                column = pl.multiple_of((xx * nz + zz) * 256, 256)
-                down_flat[:, pl.ds(column, 256)] = jnp.concatenate(
-                    [down_all[0, xx, zz], down_all[1, xx, zz]], axis=1
-                )
-            return 0
-
-        lax.fori_loop(0, nx, flatten, 0)
+        flatten(other)
         lowered = lax.dot_general(
             down_flat[...], x_v[...], NT, preferred_element_type=F32
         ).astype(BF16)
@@ -377,9 +378,10 @@
     nothing = jnp.zeros_like(new_down)
     first = jnp.concatenate([new_down, nothing], axis=0)
     second = jnp.concatenate([nothing, new_down], axis=0)
-    tz[0] = lax.dot_general(
+    rows_low = lax.dot_general(
         ctx_v[0:16], first, NT, preferred_element_type=F32
     ) + lax.dot_general(ctx_v[16:32], second, NT, preferred_element_type=F32)
+    tz[0] = rows_low.astype(BF16)
     start(low_z, decoded)
 
     @pl.when(learner)
@@ -391,7 +393,7 @@
         start(up_g, [])
 
     arrive(low_z)
-    txy[0] = jnp.sum(tz[...], axis=0)
+    txy[0] = jnp.sum(tz[...].astype(F32), axis=0).astype(BF16)
     start(low_xy, decoded)
 
     @pl.when(learner)
@@ -434,7 +436,7 @@
             axis=0,
         ).astype(BF16)
     arrive(low_xy)
-    lowered_rows = jnp.sum(txy[...], axis=0).astype(BF16)
+    lowered_rows = jnp.sum(txy[...].astype(F32), axis=0).astype(BF16)
     delta = jnp.dot(lowered_rows, squares[...], preferred_element_type=F32)
     for zz in range(nz):
         part = slice(zz * 128, (zz + 1) * 128)
@@ -496,8 +498,8 @@
         ]
     scratch += [
         pltpu.VMEM((64, 128), BF16),
-        pltpu.VMEM((nz, 16, 128), F32),
-        pltpu.VMEM((xy + 1, 16, 128), F32),
+        pltpu.VMEM((nz, 16, 128), BF16),
+        pltpu.VMEM((xy + 1, 16, 128), BF16),
         pltpu.VMEM((nz, 16, 128), BF16),
         pltpu.VMEM((nz, 16, 128), BF16),
         pltpu.VMEM((nz, 32, 128), BF16),

time: 61.9 us -> 61.3 us (level)
  no operation moved by 1% of the time
where the time goes in v6:
time: 61.3 us; the launch traced here: 61.1 us
  Pallas kernels  60.5 us (99%)
  between operations  0.64 us (1%)
    pallas_call x1, Pallas kernels, per_device(): pl.pallas_call(functools.partial(kernel, sizes, rates), out_shape=(jax.Sh...  58.7 us
    pallas_call x1, Pallas kernels, per_device(): pl.pallas_call(finish, out_shape=(jax.ShapeDtypeStruct((64, 128), BF16),...  1.85 us

profile of v6, /device:TPU:56, one launch (start us, length us, event | category | flops | bytes accessed | tf_op | source)
XLA Modules:
  0.0 61.1 jit_solution(15918297808497532204)
XLA Ops:
  0.6 58.7 %lora_step.1 = (bf16[96,128]{1,0:T(8,128)(2,1)}, bf16[2,4,8,16,128]{4,3,2,1,0:T(8,128)(2,1)}) custom-call(bf16[128,8192]{1,0:T(8,128)(2,1)} %bitcast.7, bf16[128,4096]{1,0:T(8,128)(2,1)} %bitcast.8, f32[64,128]{1,0:T(8,128)} %bitcast.10, f32[64,64]{1,0:T(8,128)} %up_hbm.1, bf16[128,4096]{1,0:T(8,128)(2,1)} %w_hbm.1, bf16[32,128]{1,0:T(8,128)(2,1)} %bitcast.11, ...), custom_call_target="tpu_custom_call" | custom-call | tf_op jit(solution)/shard_map/lora_step/pallas_call | solution.py:513
  59.3 1.9 %finish.1 = (bf16[64,128]{1,0:T(8,128)(2,1)}, bf16[64,64]{1,0:T(8,128)(2,1)}, bf16[32,4096]{1,0:T(8,128)(2,1)}) custom-call(bf16[96,128]{1,0:T(8,128)(2,1)} %get-tuple-element.8.fresh_ref, bf16[2,4,8,16,128]{4,3,2,1,0:T(8,128)(2,1)} %get-tuple-element.9.outs_ref), custom_call_target="tpu_custom_call" | custom-call | tf_op jit(solution)/shard_map/finish/pallas_call | solution.py:530

commit v7 on v6

--- a/solution.py
+++ b/solution.py
@@ -242,6 +242,9 @@
 
     local[0].wait()
     packed = packed_up()
+    local[1].wait()
+    up_all[y, x, z] = packed.astype(BF16)
+    down_all[y, x, z] = down_v[...].astype(BF16)
     pl.semaphore_wait(
         barrier,
         len(peers) + jnp.where(learner, 0, 1) + jnp.where(helper, nx - 1, 0),
@@ -253,14 +256,10 @@
             ready_sem, inc=1, device_id={"group": 0}, device_id_type=pl.DeviceIdType.MESH
         )
 
-    local[1].wait()
-
     @pl.when(jnp.logical_or(learner, helper))
     def _():
-        up_all[y, x, z] = packed.astype(BF16)
         for copy in up_z:
             copy.start()
-        down_all[y, x, z] = down_v[...].astype(BF16)
         for copy in down_z:
             copy.start()
         arrive(up_z)
@@ -287,10 +286,10 @@
     lent.extend(up_z + down_z)
     local[2].wait()
     local[3].wait()
-    lax.fori_loop(0, nx, project, 0)
 
     @pl.when(jnp.logical_not(learner))
     def _():
+        lax.fori_loop(0, nx, project, 0)
         start(base_xy, [])
         base_lines()
         base_total()
@@ -325,6 +324,7 @@
                 gd[0, xx, zz] = block[:, 0:128]
                 gd[1, xx, zz] = block[:, 128:256]
             start([c for c, p in zip(gd_xy, plane) if p[0] == dx], learnt)
+        lax.fori_loop(0, nx, project, 0)
         start(base_xy, [])
         def flatten(plane_y):
             for xx in range(nx):
@@ -392,6 +392,11 @@
         start(up_spread, learnt)
         start(up_g, [])
 
+    @pl.when(jnp.logical_not(learner))
+    def _():
+        up_spread[0].wait_recv()
+        start(up_g, [])
+
     arrive(low_z)
     txy[0] = jnp.sum(tz[...].astype(F32), axis=0).astype(BF16)
     start(low_xy, decoded)
@@ -399,11 +404,6 @@
     @pl.when(learner)
     def _():
         freeze()
-
-    @pl.when(jnp.logical_not(learner))
-    def _():
-        up_spread[0].wait_recv()
-        start(up_g, [])
 
     written = [
         pltpu.make_async_copy(fresh, new_hbm.at[0:64], local_sem.at[8]),
@@ -421,12 +421,11 @@
     def _():
         sent(lent)
 
-    arrive(up_g)
-    for zz in range(nz):
+    def square(zz):
         new_up = up_line[zz].astype(F32)
         turned = pltpu.roll(new_up, 64, 1)
         keep = left_half(new_up.shape)
-        squares[:, zz * 128 : (zz + 1) * 128] = jnp.concatenate(
+        squares[:, pl.ds(pl.multiple_of(zz * 128, 128), 128)] = jnp.concatenate(
             [
                 jnp.where(keep, new_up, 0.0),
                 jnp.where(keep, turned, 0.0),
@@ -435,6 +434,11 @@
             ],
             axis=0,
         ).astype(BF16)
+
+    square(z)
+    for d, copy in zip(line[::-1], up_g[::-1]):
+        arrive([copy])
+        square(lax.rem(z + nz - d, nz))
     arrive(low_xy)
     lowered_rows = jnp.sum(txy[...].astype(F32), axis=0).astype(BF16)
     delta = jnp.dot(lowered_rows, squares[...], preferred_element_type=F32)

time: 61.3 us -> 60.8 us (level)
  Pallas kernels: 60.5 us -> 59.8 us
    pallas_call x1, Pallas kernels: 58.7 us -> 58 us  [per_device(): pl.pallas_call(functools.partial(kernel, sizes, rates), out_shape=(jax.Sh...]
where the time goes in v7:
time: 60.8 us; the launch traced here: 60.5 us
  Pallas kernels  59.8 us (98%)
  between operations  0.64 us (1%)
    pallas_call x1, Pallas kernels, per_device(): pl.pallas_call(functools.partial(kernel, sizes, rates), out_shape=(jax.Sh...  58 us
    pallas_call x1, Pallas kernels, per_device(): pl.pallas_call(finish, out_shape=(jax.ShapeDtypeStruct((64, 128), BF16),...  1.85 us

profile of v7, /device:TPU:56, one launch (start us, length us, event | category | flops | bytes accessed | tf_op | source)
XLA Modules:
  0.0 60.5 jit_solution(10914744234953715785)
XLA Ops:
  0.6 58.0 %lora_step.1 = (bf16[96,128]{1,0:T(8,128)(2,1)}, bf16[2,4,8,16,128]{4,3,2,1,0:T(8,128)(2,1)}) custom-call(bf16[128,8192]{1,0:T(8,128)(2,1)} %bitcast.7, bf16[128,4096]{1,0:T(8,128)(2,1)} %bitcast.8, f32[64,128]{1,0:T(8,128)} %bitcast.10, f32[64,64]{1,0:T(8,128)} %up_hbm.1, bf16[128,4096]{1,0:T(8,128)(2,1)} %w_hbm.1, bf16[32,128]{1,0:T(8,128)(2,1)} %bitcast.11, ...), custom_call_target="tpu_custom_call" | custom-call | tf_op jit(solution)/shard_map/lora_step/pallas_call | solution.py:517
  58.6 1.9 %finish.1 = (bf16[64,128]{1,0:T(8,128)(2,1)}, bf16[64,64]{1,0:T(8,128)(2,1)}, bf16[32,4096]{1,0:T(8,128)(2,1)}) custom-call(bf16[96,128]{1,0:T(8,128)(2,1)} %get-tuple-element.8.fresh_ref, bf16[2,4,8,16,128]{4,3,2,1,0:T(8,128)(2,1)} %get-tuple-element.9.outs_ref), custom_call_target="tpu_custom_call" | custom-call | tf_op jit(solution)/shard_map/finish/pallas_call | solution.py:534
